TPU v7x, 128 devices: a whole 4x4x4 slice. The times are simulated.
128 devices in a mesh: gx: 16 (over z_hi, y, core), gy: 8 (over z_lo, x).
Axes of the slice: x: 4, y: 4, z: 4 (z_hi: 2, z_lo: 2; z = z_hi * 2 + z_lo), core: 2. Of those that a mesh axis runs over, the one named last changes fastest.
Arguments:
- pressure: float32 [512, 256, 256], P('gx', 'gy'), may hold values from -6 to 6
- previous: float32 [512, 256, 256], P('gx', 'gy'), may hold values from -6 to 6
- courant: float32 [512, 256, 256], P('gx', 'gy'), may hold values from 0.05 to 0.2
- snapshots: float32 [4, 512, 256, 256], P(None, 'gx', 'gy'), may hold values from -6 to 6
- traces: float32 [128, 128, 4, 128], P(('gx', 'gy')), may hold values from -6 to 6
- cell_offsets: int32 [128, 128, 128], P(('gx', 'gy')), may hold values from 0 to 262143
- live_counts: int32 [128, 128], P(('gx', 'gy')), may hold values from 0 to 128, as said below
Outputs:
- final_pressure: float32 [512, 256, 256], P('gx', 'gy')
- final_previous: float32 [512, 256, 256], P('gx', 'gy')
- image: float32 [512, 256, 256], P('gx', 'gy')
Inputs may be any that keep to these rules, and one draw needn't show every extreme that they name: live_counts[s, d] is the number of live slots from device s to subdomain d; in every draw some subdomain receives 128 live slots from every device.
All inputs are finite; a program needn't handle non-finite values.
Results may differ from a plain program's by a relative error of at most 0.00002.
Values sent between devices are 32-bit elements; how exact they have to be, the bound alone decides.
A program may use at most 64 MiB of HBM per device.

v0:
```python
import jax
import jax.numpy as jnp
from jax import lax
from jax.sharding import PartitionSpec as P

STEPS = 4


COEFS = (-205.0 / 72.0, 8.0 / 5.0, -1.0 / 5.0, 8.0 / 315.0, -1.0 / 560.0)


def extended(block, sides, width):
    for axis, dim in sides:
        count = lax.axis_size(axis)
        forward = [(i, i + 1) for i in range(count - 1)]
        backward = [(target, source) for source, target in forward]
        low = lax.ppermute(
            lax.slice_in_dim(block, block.shape[dim] - width, None, axis=dim), axis, forward
        )
        high = lax.ppermute(lax.slice_in_dim(block, 0, width, axis=dim), axis, backward)
        block = jnp.concatenate([low, block, high], axis=dim)
    return block


def stencil(padded, width_x, width_y, depth):
    centre = padded[4 : 4 + width_x, 4 : 4 + width_y, 4 : 4 + depth]
    total = 3.0 * COEFS[0] * centre
    for shift in range(1, 5):
        pairs = padded[4 + shift : 4 + shift + width_x, 4 : 4 + width_y, 4 : 4 + depth]
        pairs = pairs + padded[4 - shift : 4 - shift + width_x, 4 : 4 + width_y, 4 : 4 + depth]
        pairs = pairs + padded[4 : 4 + width_x, 4 + shift : 4 + shift + width_y, 4 : 4 + depth]
        pairs = pairs + padded[4 : 4 + width_x, 4 - shift : 4 - shift + width_y, 4 : 4 + depth]
        pairs = pairs + padded[4 : 4 + width_x, 4 : 4 + width_y, 4 + shift : 4 + shift + depth]
        pairs = pairs + padded[4 : 4 + width_x, 4 : 4 + width_y, 4 - shift : 4 - shift + depth]
        total = total + COEFS[shift] * pairs
    return total


def extend(field):
    wider = extended(field, (("gx", 0), ("gy", 1)), 4)
    return jnp.pad(wider, ((0, 0), (0, 0), (4, 4)))


def local(pressure, previous, courant, snapshots, traces, cell_offsets, live_counts):
    width_x, width_y, depth = pressure.shape
    slots = traces.shape[3]
    slot = jnp.arange(slots, dtype=jnp.int32)
    live = slot[None, None, :] < live_counts[:, :, None]
    masked = jnp.where(live[:, :, None, :], traces, jnp.float32(0.0))
    arrived_cells = lax.all_to_all(
        cell_offsets, ("gx", "gy"), split_axis=1, concat_axis=0, tiled=True
    ).reshape(-1)
    image = jnp.zeros(pressure.shape, jnp.float32)
    for step in range(STEPS):
        padded = extend(pressure)
        nxt = 2.0 * pressure - previous + courant * stencil(padded, width_x, width_y, depth)
        values = lax.all_to_all(
            masked[:, :, step, :], ("gx", "gy"), split_axis=1, concat_axis=0, tiled=True
        ).reshape(-1)
        nxt = nxt.reshape(-1).at[arrived_cells].add(values).reshape(pressure.shape)
        image = image + snapshots[step] * nxt
        previous = pressure
        pressure = nxt
    return (pressure, previous, image)


def solution(mesh):
    placed = (
        P("gx", "gy", None),
        P("gx", "gy", None),
        P("gx", "gy", None),
        P(None, "gx", "gy", None),
        P(("gx", "gy"), None, None, None),
        P(("gx", "gy"), None, None),
        P(("gx", "gy"), None),
    )
    return jax.shard_map(
        local,
        mesh=mesh,
        in_specs=placed,
        out_specs=(P("gx", "gy", None), P("gx", "gy", None), P("gx", "gy", None)),
        check_vma=False,
    )
```

profile of v0, /device:TPU:6, one launch (start us, length us, event | category | flops | bytes accessed | tf_op | source)
XLA Modules:
  0.0 536.6 jit_solution(15284898833362549193)
XLA Ops:
  0.6 10.5 %all-to-all-start = ((s32[1,128,128]{2,0,1:T(1,128)}), s32[1,128,128]{2,0,1:T(1,128)S(1)}, u32[]{:S(2)}, u32[]{:S(2)}) async-start(s32[1,128,128]{2,0,1:T(1,128)} %bitcast.65), calls=%async_computation | async-start | bytes 131072 | tf_op jit(solution)/shard_map/all_to_all | solution.py:50
  13.4 3.0 collective-permute-start.1
  21.2 2.8 collective-permute-start.2
  23.9 5.2 collective-permute-start.3
  29.8 14.0 %all-to-all-start.1 = ((f32[1,128,128]{2,0,1:T(1,128)}), f32[1,128,128]{2,0,1:T(1,128)S(1)}, u32[]{:S(2)}, u32[]{:S(2)}) async-start(f32[1,128,128]{2,0,1:T(1,128)} %bitcast.64), calls=%async_computation.1 | async-start | bytes 131072 | tf_op jit(solution)/shard_map/all_to_all | solution.py:57
  44.8 2.6 select_maximum_fusion.6
  47.5 4.9 fusion.90
  52.9 88.2 %scatter_fusion = f32[262144]{0:T(1024)S(1)} fusion(f32[262144]{0:T(1024)S(1)} %bitcast.47, s32[16384]{0:T(1024)S(1)} %bitcast.55, f32[16384]{0:T(1024)S(1)} %bitcast.59), kind=kCustom, calls=%fused_computation | custom fusion | flops 16384 | bytes 262144 | tf_op jit(solution)/shard_map/scatter-add | solution.py:60
  141.2 2.1 collective-permute-start.5
  145.9 2.7 collective-permute-done.4
  150.6 2.8 collective-permute-start.6
  153.3 5.2 collective-permute-start.7
  158.5 14.4 %all-to-all-start.2 = ((f32[1,128,128]{2,0,1:T(1,128)}), f32[1,128,128]{2,0,1:T(1,128)S(1)}, u32[]{:S(2)}, u32[]{:S(2)}) async-start(f32[1,128,128]{2,0,1:T(1,128)} %bitcast.63), calls=%async_computation.2 | async-start | bytes 131072 | tf_op jit(solution)/shard_map/all_to_all | solution.py:57
  172.9 2.6 select_maximum_fusion.4
  175.6 4.9 fusion.63
  181.1 88.2 %scatter_fusion.1 = f32[262144]{0:T(1024)S(1)} fusion(f32[262144]{0:T(1024)S(1)} %bitcast.48, s32[16384]{0:T(1024)S(1)} %bitcast.56, f32[16384]{0:T(1024)S(1)} %bitcast.61), kind=kCustom, calls=%fused_computation.1 | custom fusion | flops 16384 | bytes 262144 | tf_op jit(solution)/shard_map/scatter-add | solution.py:60
  270.0 2.7 collective-permute-start.9
  280.0 2.8 collective-permute-start.10
  282.8 5.2 collective-permute-start.11
  287.9 14.4 %all-to-all-start.3 = ((f32[1,128,128]{2,0,1:T(1,128)}), f32[1,128,128]{2,0,1:T(1,128)S(1)}, u32[]{:S(2)}, u32[]{:S(2)}) async-start(f32[1,128,128]{2,0,1:T(1,128)} %bitcast.10), calls=%async_computation.3 | async-start | bytes 131072 | tf_op jit(solution)/shard_map/all_to_all | solution.py:57
  302.4 2.6 select_maximum_fusion.2
  305.0 5.6 %fusion.36 = f32[32,32,256]{2,1,0:T(8,128)S(1)} fusion(f32[32,32,256]{2,1,0:T(8,128)S(1)} %copy-done.2, f32[40,32,256]{2,1,0:T(8,128)S(1)} %copy-done.12, f32[40,4,256]{2,1,0:T(4,128)} %collective-permute-done.11, f32[40,4,256]{2,1,0:T(4,128)} %collective-permute-done.10, f32[40,40,264]{2,1,0:T(8,128)S(1)} %select_maximum_fusion.2, ...), kind=kLoop, calls=%fused_computation.98 | loop fusion | flops 10747904 | bytes 22609920 | tf_op jit(solution)/shard_map/add | solution.py:56
  311.2 88.2 %scatter_fusion.2 = f32[262144]{0:T(1024)S(1)} fusion(f32[262144]{0:T(1024)S(1)} %bitcast.49, s32[16384]{0:T(1024)S(1)} %bitcast.57, f32[16384]{0:T(1024)S(1)} %bitcast.62), kind=kCustom, calls=%fused_computation.2 | custom fusion | flops 16384 | bytes 262144 | tf_op jit(solution)/shard_map/scatter-add | solution.py:60
  400.2 2.7 collective-permute-start.13
  407.3 2.5 constant_dynamic-update-slice_fusion.22
  412.3 2.8 collective-permute-start.14
  415.1 5.2 collective-permute-start.15
  420.3 13.1 %all-to-all-start.4 = ((f32[1,128,128]{2,0,1:T(1,128)}), f32[1,128,128]{2,0,1:T(1,128)S(1)}, u32[]{:S(2)}, u32[]{:S(2)}) async-start(f32[1,128,128]{2,0,1:T(1,128)} %bitcast.13), calls=%async_computation.4 | async-start | bytes 131072 | tf_op jit(solution)/shard_map/all_to_all | solution.py:57
  433.5 2.6 select_maximum_fusion
  436.1 5.6 %fusion.9 = f32[32,32,256]{2,1,0:T(8,128)S(1)} fusion(f32[32,32,256]{2,1,0:T(8,128)S(1)} %copy-done.3, f32[40,32,256]{2,1,0:T(8,128)S(1)} %copy-done.14, f32[40,4,256]{2,1,0:T(4,128)} %collective-permute-done.15, f32[40,4,256]{2,1,0:T(4,128)} %collective-permute-done.14, f32[40,40,264]{2,1,0:T(8,128)S(1)} %select_maximum_fusion, ...), kind=kLoop, calls=%fused_computation.71 | loop fusion | flops 10747904 | bytes 22609920 | tf_op jit(solution)/shard_map/add | solution.py:56
  442.4 88.2 %scatter_fusion.3 = f32[262144]{0:T(1024)S(1)} fusion(f32[262144]{0:T(1024)S(1)} %bitcast.50, s32[16384]{0:T(1024)S(1)} %bitcast.58, f32[16384]{0:T(1024)S(1)} %bitcast.60), kind=kCustom, calls=%fused_computation.3 | custom fusion | flops 16384 | bytes 262144 | tf_op jit(solution)/shard_map/scatter-add | solution.py:60
  531.8 4.7 fusion.121
  (95 shorter events, 32.1 us)
Async XLA Ops:
  0.6 18.3 %copy-start.5 = (f32[32,32,256]{2,1,0:T(8,128)S(1)}, f32[32,32,256]{2,1,0:T(8,128)}, u32[]{:S(2)}) copy-start(f32[32,32,256]{2,1,0:T(8,128)} %param.7) | copy-start | bytes 3145732
  0.6 28.5 %all-to-all-start = ((s32[1,128,128]{2,0,1:T(1,128)}), s32[1,128,128]{2,0,1:T(1,128)S(1)}, u32[]{:S(2)}, u32[]{:S(2)}) async-start(s32[1,128,128]{2,0,1:T(1,128)} %bitcast.65), calls=%async_computation | async-start | bytes 131072 | tf_op jit(solution)/shard_map/all_to_all | solution.py:50
  12.1 7.2 %collective-permute-start = (f32[4,32,256]{2,1,0:T(8,128)S(1)}, f32[4,32,256]{2,1,0:T(8,128)S(1)}, u32[]{:S(2)}, u32[]{:S(2)}) collective-permute-start(f32[4,32,256]{2,1,0:T(8,128)S(1)} %get-tuple-element.29), channel_id=1, source_target_pairs={{8,0},{16,8},{24,16},{32,24},{40,32},{48,40},{56,48},{64,56},{72,6... | collective-permute-start | bytes 393224 | tf_op jit(solution)/shard_map/ppermute | solution.py:20
  13.4 5.5 %collective-permute-start.1 = (f32[4,32,256]{2,1,0:T(8,128)S(1)}, f32[4,32,256]{2,1,0:T(8,128)S(1)}, u32[]{:S(2)}, u32[]{:S(2)}) collective-permute-start(f32[4,32,256]{2,1,0:T(8,128)S(1)} %get-tuple-element.30), channel_id=1, source_target_pairs={{0,8},{8,16},{16,24},{24,32},{32,40},{40,48},{48,56},{56,64},{64,7... | collective-permute-start | bytes 393224 | tf_op jit(solution)/shard_map/ppermute | solution.py:17
  21.2 23.6 %collective-permute-start.2 = (f32[40,4,256]{2,1,0:T(4,128)}, f32[40,4,256]{2,1,0:T(4,128)}, u32[]{:S(2)}, u32[]{:S(2)}) collective-permute-start(f32[40,4,256]{2,1,0:T(4,128)} %get-tuple-element.9), channel_id=1, source_target_pairs={{1,0},{2,1},{3,2},{4,3},{5,4},{6,5},{7,6},{9,8},{10,9},{11,10},{12... | collective-permute-start | bytes 491528 | tf_op jit(solution)/shard_map/ppermute | solution.py:20
  23.9 20.9 %collective-permute-start.3 = (f32[40,4,256]{2,1,0:T(4,128)}, f32[40,4,256]{2,1,0:T(4,128)}, u32[]{:S(2)}, u32[]{:S(2)}) collective-permute-start(f32[40,4,256]{2,1,0:T(4,128)} %get-tuple-element.10), channel_id=1, source_target_pairs={{0,1},{1,2},{2,3},{3,4},{4,5},{5,6},{6,7},{8,9},{9,10},{10,11},{11... | collective-permute-start | bytes 491528 | tf_op jit(solution)/shard_map/ppermute | solution.py:17
  29.8 23.1 %all-to-all-start.1 = ((f32[1,128,128]{2,0,1:T(1,128)}), f32[1,128,128]{2,0,1:T(1,128)S(1)}, u32[]{:S(2)}, u32[]{:S(2)}) async-start(f32[1,128,128]{2,0,1:T(1,128)} %bitcast.64), calls=%async_computation.1 | async-start | bytes 131072 | tf_op jit(solution)/shard_map/all_to_all | solution.py:57
  44.7 2.7 copy-start
  44.8 2.7 copy-start.8
  44.8 2.7 copy-start.15
  141.2 4.4 collective-permute-start.5
  144.3 4.4 collective-permute-start.4
  150.6 22.4 %collective-permute-start.6 = (f32[40,4,256]{2,1,0:T(4,128)}, f32[40,4,256]{2,1,0:T(4,128)}, u32[]{:S(2)}, u32[]{:S(2)}) collective-permute-start(f32[40,4,256]{2,1,0:T(4,128)} %get-tuple-element.7), channel_id=1, source_target_pairs={{1,0},{2,1},{3,2},{4,3},{5,4},{6,5},{7,6},{9,8},{10,9},{11,10},{12... | collective-permute-start | bytes 491528 | tf_op jit(solution)/shard_map/ppermute | solution.py:20
  153.3 19.6 %collective-permute-start.7 = (f32[40,4,256]{2,1,0:T(4,128)}, f32[40,4,256]{2,1,0:T(4,128)}, u32[]{:S(2)}, u32[]{:S(2)}) collective-permute-start(f32[40,4,256]{2,1,0:T(4,128)} %get-tuple-element.8), channel_id=1, source_target_pairs={{0,1},{1,2},{2,3},{3,4},{4,5},{5,6},{6,7},{8,9},{9,10},{10,11},{11... | collective-permute-start | bytes 491528 | tf_op jit(solution)/shard_map/ppermute | solution.py:17
  158.5 22.5 %all-to-all-start.2 = ((f32[1,128,128]{2,0,1:T(1,128)}), f32[1,128,128]{2,0,1:T(1,128)S(1)}, u32[]{:S(2)}, u32[]{:S(2)}) async-start(f32[1,128,128]{2,0,1:T(1,128)} %bitcast.63), calls=%async_computation.2 | async-start | bytes 131072 | tf_op jit(solution)/shard_map/all_to_all | solution.py:57
  172.9 2.7 copy-start.1
  172.9 2.7 copy-start.6
  172.9 2.7 copy-start.10
  270.0 5.0 collective-permute-start.9
  273.7 3.7 collective-permute-start.8
  280.0 22.4 %collective-permute-start.10 = (f32[40,4,256]{2,1,0:T(4,128)}, f32[40,4,256]{2,1,0:T(4,128)}, u32[]{:S(2)}, u32[]{:S(2)}) collective-permute-start(f32[40,4,256]{2,1,0:T(4,128)} %get-tuple-element.5), channel_id=1, source_target_pairs={{1,0},{2,1},{3,2},{4,3},{5,4},{6,5},{7,6},{9,8},{10,9},{11,10},{12... | collective-permute-start | bytes 491528 | tf_op jit(solution)/shard_map/ppermute | solution.py:20
  282.8 19.6 %collective-permute-start.11 = (f32[40,4,256]{2,1,0:T(4,128)}, f32[40,4,256]{2,1,0:T(4,128)}, u32[]{:S(2)}, u32[]{:S(2)}) collective-permute-start(f32[40,4,256]{2,1,0:T(4,128)} %get-tuple-element.6), channel_id=1, source_target_pairs={{0,1},{1,2},{2,3},{3,4},{4,5},{5,6},{6,7},{8,9},{9,10},{10,11},{11... | collective-permute-start | bytes 491528 | tf_op jit(solution)/shard_map/ppermute | solution.py:17
  287.9 23.3 %all-to-all-start.3 = ((f32[1,128,128]{2,0,1:T(1,128)}), f32[1,128,128]{2,0,1:T(1,128)S(1)}, u32[]{:S(2)}, u32[]{:S(2)}) async-start(f32[1,128,128]{2,0,1:T(1,128)} %bitcast.10), calls=%async_computation.3 | async-start | bytes 131072 | tf_op jit(solution)/shard_map/all_to_all | solution.py:57
  302.3 2.7 copy-start.2
  400.2 6.2 %collective-permute-start.13 = (f32[4,32,256]{2,1,0:T(8,128)}, f32[4,32,256]{2,1,0:T(8,128)}, u32[]{:S(2)}, u32[]{:S(2)}) collective-permute-start(f32[4,32,256]{2,1,0:T(8,128)} %slice.693), channel_id=1, source_target_pairs={{0,8},{8,16},{16,24},{24,32},{32,40},{40,48},{48,56},{56,64},{64,7... | collective-permute-start | bytes 393224 | tf_op jit(solution)/shard_map/ppermute | solution.py:17
  404.8 5.0 collective-permute-start.12
  412.3 21.1 %collective-permute-start.14 = (f32[40,4,256]{2,1,0:T(4,128)}, f32[40,4,256]{2,1,0:T(4,128)}, u32[]{:S(2)}, u32[]{:S(2)}) collective-permute-start(f32[40,4,256]{2,1,0:T(4,128)} %get-tuple-element.3), channel_id=1, source_target_pairs={{1,0},{2,1},{3,2},{4,3},{5,4},{6,5},{7,6},{9,8},{10,9},{11,10},{12... | collective-permute-start | bytes 491528 | tf_op jit(solution)/shard_map/ppermute | solution.py:20
  415.1 18.4 %collective-permute-start.15 = (f32[40,4,256]{2,1,0:T(4,128)}, f32[40,4,256]{2,1,0:T(4,128)}, u32[]{:S(2)}, u32[]{:S(2)}) collective-permute-start(f32[40,4,256]{2,1,0:T(4,128)} %get-tuple-element.4), channel_id=1, source_target_pairs={{0,1},{1,2},{2,3},{3,4},{4,5},{5,6},{6,7},{8,9},{9,10},{10,11},{11... | collective-permute-start | bytes 491528 | tf_op jit(solution)/shard_map/ppermute | solution.py:17
  420.3 22.0 %all-to-all-start.4 = ((f32[1,128,128]{2,0,1:T(1,128)}), f32[1,128,128]{2,0,1:T(1,128)S(1)}, u32[]{:S(2)}, u32[]{:S(2)}) async-start(f32[1,128,128]{2,0,1:T(1,128)} %bitcast.13), calls=%async_computation.4 | async-start | bytes 131072 | tf_op jit(solution)/shard_map/all_to_all | solution.py:57
  433.4 2.7 copy-start.3
  433.4 2.7 copy-start.4
  433.4 2.7 copy-start.14
  (6 other events, 7.7 us)
where the time goes:
time: 539 us; the launch traced here: 537 us
  other arithmetic  392 us (73%)
  starting transfers between devices  114 us (21%)
  local copies, waits for them, and re-layouts  26.4 us (5%)
    scatter-add x4, other arithmetic, local(): nxt = nxt.reshape(-1).at[arrived_cells].add(values).reshape(pressure.shape)  353 us
    all_to_all x4, starting transfers between devices, local(): lax.all_to_all(masked[:, :, step, :], ('gx', 'gy'), split_axis=1, concat_...  55.9 us
    ppermute x8, starting transfers between devices, extended(): lax.ppermute(lax.slice_in_dim(block, block.shape[dim] - width, None, axis...  31.3 us
    add x4, other arithmetic, local(): 2.0 * pressure - previous  21.1 us
    ppermute x8, starting transfers between devices, extended(): lax.ppermute(lax.slice_in_dim(block, 0, width, axis=dim), axis, backward)  16.4 us
    unnamed x46, local copies, waits for them, and re-layouts  13.5 us
  transfers between devices with their start and end apart: 21, of which 2 were waited for; matrix products, arithmetic and copies ran while one was open for 9% of the time, Pallas kernels for 0%

commit v1 on v0

v1 whole, which is shorter than its diff:
```python
import functools

import jax
import jax.numpy as jnp
from jax import lax
from jax.experimental import pallas as pl
from jax.experimental.pallas import tpu as pltpu
from jax.sharding import PartitionSpec as P

STEPS = 4
COEFS = (-205.0 / 72.0, 8.0 / 5.0, -1.0 / 5.0, 8.0 / 315.0, -1.0 / 560.0)
NX, NY = 16, 8
K = 5
ROWS = 8192 + 16
MESH = pl.DeviceIdType.MESH
FIELD = (40, 2, 48, 128)
BLOCK = (32, 2, 32, 128)


def barrier(peers):
    sem = pltpu.get_barrier_semaphore()
    for axis, device in peers:
        pl.semaphore_signal(sem, inc=1, device_id={axis: device}, device_id_type=MESH)
    pl.semaphore_wait(sem, len(peers))


def z_matrix():
    row = lax.broadcasted_iota(jnp.int32, (256, 256), 0)
    col = lax.broadcasted_iota(jnp.int32, (256, 256), 1)
    apart = jnp.abs(row - col)
    matrix = jnp.where(apart == 0, 3.0 * COEFS[0], 0.0)
    for shift in range(1, 5):
        matrix = jnp.where(apart == shift, COEFS[shift], matrix)
    return matrix.astype(jnp.float32)


def z_terms(field, dz, zterm):
    def body(i, _):
        xs = pl.ds(4 + i * 8, 8)
        left = field[xs, 0, pl.ds(8, 32), :].reshape(256, 128)
        right = field[xs, 1, pl.ds(8, 32), :].reshape(256, 128)
        both = jnp.concatenate([left, right], axis=1)
        out = jnp.dot(both, dz[...], precision=lax.Precision.HIGHEST, preferred_element_type=jnp.float32)
        zterm[pl.ds(i * 8, 8), 0] = out[:, :128].reshape(8, 32, 128)
        zterm[pl.ds(i * 8, 8), 1] = out[:, 128:].reshape(8, 32, 128)
        return 0

    lax.fori_loop(0, 4, body, 0)


def laplacian(field, zterm, x, half, tile):
    rows = 8 + tile * 8
    total = zterm[x, half, pl.ds(tile * 8, 8), :]
    for shift in range(1, 5):
        pairs = field[x + 4 + shift, half, pl.ds(rows, 8), :] + field[x + 4 - shift, half, pl.ds(rows, 8), :]
        pairs = pairs + field[x + 4, half, pl.ds(rows + shift, 8), :]
        pairs = pairs + field[x + 4, half, pl.ds(rows - shift, 8), :]
        total = total + COEFS[shift] * pairs
    return total


class Halo:
    def __init__(self, field, ysend, yrecv, sems, index):
        a, b = lax.axis_index("gx"), lax.axis_index("gy")
        self.field, self.ysend, self.yrecv = field, ysend, yrecv
        self.there = (b > 0, b < NY - 1, a > 0, a < NX - 1)
        self.come = (b < NY - 1, b > 0, a < NX - 1, a > 0)
        send, recv = sems

        def copy(d, src, dst, axis, device):
            return pltpu.make_async_remote_copy(
                src_ref=src, dst_ref=dst, send_sem=send.at[index, d], recv_sem=recv.at[index, d],
                device_id={axis: device}, device_id_type=MESH,
            )

        ys = pl.ds(8, 32)
        self.copies = (
            copy(0, ysend.at[0], yrecv.at[0], "gy", b - 1),
            copy(1, ysend.at[1], yrecv.at[1], "gy", b + 1),
            copy(2, field.at[pl.ds(4, 4), :, ys, :], field.at[pl.ds(36, 4), :, ys, :], "gx", a - 1),
            copy(3, field.at[pl.ds(32, 4), :, ys, :], field.at[pl.ds(0, 4), :, ys, :], "gx", a + 1),
        )

    def start(self, d):
        pl.when(self.there[d])(lambda: self.copies[d].start())

    def start_y(self):
        def body(x, _):
            for half in range(2):
                self.ysend[0, x, half] = self.field[x + 4, half, pl.ds(8, 4), :]
                self.ysend[1, x, half] = self.field[x + 4, half, pl.ds(36, 4), :]
            return 0

        lax.fori_loop(0, 32, body, 0)
        self.start(0)
        self.start(1)

    def start_x(self):
        self.start(2)
        self.start(3)

    def wait(self):
        for d in range(4):
            pl.when(self.come[d])(lambda: self.copies[d].wait_recv())
        for d in range(4):
            pl.when(self.there[d])(lambda: self.copies[d].wait_send())

        def body(x, _):
            for half in range(2):
                self.field[x + 4, half, pl.ds(40, 4), :] = self.yrecv[0, x, half]
                self.field[x + 4, half, pl.ds(4, 4), :] = self.yrecv[1, x, half]
            return 0

        lax.fori_loop(0, 32, body, 0)


def clear_edges(field, yrecvs):
    a, b = lax.axis_index("gx"), lax.axis_index("gy")

    @pl.when(a == 0)
    def _():
        field[pl.ds(0, 4)] = jnp.zeros((4,) + FIELD[1:], jnp.float32)

    @pl.when(a == NX - 1)
    def _():
        field[pl.ds(36, 4)] = jnp.zeros((4,) + FIELD[1:], jnp.float32)

    for yrecv in yrecvs:
        @pl.when(b == NY - 1)
        def _():
            yrecv[0] = jnp.zeros((32, 2, 4, 128), jnp.float32)

        @pl.when(b == 0)
        def _():
            yrecv[1] = jnp.zeros((32, 2, 4, 128), jnp.float32)


def deliver_kernel(
    traces, codes, pressure, previous, courant, values_out, codes_out, hom,
    mid_values, mid_codes, field, zterm, dz, ysend, yrecv,
    local_sem, send1, recv1, send2, recv2, hsend, hrecv,
):
    a, b = lax.axis_index("gx"), lax.axis_index("gy")
    sem = pltpu.get_barrier_semaphore()
    peers = [("gy", lax.rem(b + o, NY)) for o in range(1, NY)]
    peers += [("gx", lax.rem(a + o, NX)) for o in range(1, NX)]
    for axis, device in peers:
        pl.semaphore_signal(sem, inc=1, device_id={axis: device}, device_id_type=MESH)

    def load(x, _):
        for half in range(2):
            field[x + 4, half, pl.ds(8, 32), :] = pressure[x, :, half * 128 : half * 128 + 128]
        return 0

    lax.fori_loop(0, 32, load, 0)
    clear_edges(field, [yrecv])
    pl.semaphore_wait(sem, len(peers))

    own1 = [
        pltpu.make_async_copy(traces.at[:, b], mid_values.at[b], local_sem.at[0]),
        pltpu.make_async_copy(codes.at[:, b], mid_codes.at[b], local_sem.at[1]),
    ]
    stage1 = []
    for o in range(1, NY):
        to = lax.rem(b + o, NY)
        for kind, (src, dst) in enumerate(((traces, mid_values), (codes, mid_codes))):
            stage1.append(pltpu.make_async_remote_copy(
                src_ref=src.at[:, to], dst_ref=dst.at[b],
                send_sem=send1.at[o - 1, kind], recv_sem=recv1.at[o - 1, kind],
                device_id={"gy": to}, device_id_type=MESH,
            ))
    for copy in stage1:
        copy.start()
    for copy in own1:
        copy.start()
    halo = Halo(field, ysend, yrecv, (hsend, hrecv), 0)
    halo.start_y()
    halo.start_x()

    dz[...] = z_matrix()
    z_terms(field, dz, zterm)

    for copy in own1:
        copy.wait()
    for copy in stage1:
        copy.wait_recv()

    own2 = [
        pltpu.make_async_copy(mid_values.at[:, a], values_out.at[a], local_sem.at[2]),
        pltpu.make_async_copy(mid_codes.at[:, a], codes_out.at[a], local_sem.at[3]),
    ]
    stage2 = []
    for o in range(1, NX):
        to = lax.rem(a + o, NX)
        for kind, (src, dst) in enumerate(((mid_values, values_out), (mid_codes, codes_out))):
            stage2.append(pltpu.make_async_remote_copy(
                src_ref=src.at[:, to], dst_ref=dst.at[a],
                send_sem=send2.at[o - 1, kind], recv_sem=recv2.at[o - 1, kind],
                device_id={"gx": to}, device_id_type=MESH,
            ))
    for copy in stage2:
        copy.start()
    for copy in own2:
        copy.start()

    halo.wait()

    def step(x, _):
        for half in range(2):
            lanes = pl.ds(half * 128, 128)
            for tile in range(4):
                rows = pl.ds(tile * 8, 8)
                now = field[x + 4, half, pl.ds(8 + tile * 8, 8), :]
                out = 2.0 * now - previous[x, rows, lanes]
                hom[x, half, rows, :] = out + courant[x, rows, lanes] * laplacian(field, zterm, x, half, tile)
        return 0

    lax.fori_loop(0, 32, step, 0)

    for copy in stage1:
        copy.wait_send()
    for copy in own2:
        copy.wait()
    for copy in stage2:
        copy.wait()


def scatter_kernel(codes, values, hom, first, later, *sums):
    zero = jnp.zeros((64, 128), jnp.float32)

    def clear(i, _):
        for total in sums:
            total[pl.ds(pl.multiple_of(i * 64, 64), 64), :] = zero
        return 0

    lax.fori_loop(0, 128, clear, 0)
    for total in sums:
        total[pl.ds(8192, 16), :] = jnp.zeros((16, 128), jnp.float32)
    sub = lax.broadcasted_iota(jnp.int32, (8, 128), 0)
    lane = lax.broadcasted_iota(jnp.int32, (8, 128), 1)
    place = (jnp.where(sub < 4, lane, -1), jnp.where(sub < 4, -1, lane))

    def body(s, _):
        both = jnp.concatenate([values[2 * s], values[2 * s + 1]], axis=0)
        for j in range(128):
            wide = jnp.broadcast_to(both[:, j : j + 1], (8, 128))
            for h in range(2):
                code = codes[2 * s + h, j]
                rows = pl.ds(code >> 8, 8)
                cell = jnp.full((8, 128), code, jnp.int32) & 255
                total = sums[(2 * j + h) % K]
                total[rows, :] = total[rows, :] + jnp.where(place[h] == cell, wide, 0.0)
        return 0

    lax.fori_loop(0, 64, body, 0)

    def finish(i, _):
        rows = pl.ds(pl.multiple_of(i * 64 + 8, 8), 64)
        total = sums[0][rows, :]
        for other in sums[1:]:
            total = total + other[rows, :]
        turned = jnp.swapaxes(total.reshape(8, 8, 128), 0, 1)
        x, ys = i // 4, pl.ds(pl.multiple_of(i % 4 * 8, 8), 8)
        for half in range(2):
            first[x, half, ys, :] = hom[x, half, ys, :] + turned[half * 4]
            for t in range(1, STEPS):
                later[t - 1, x, half, ys, :] = turned[half * 4 + t]
        return 0

    lax.fori_loop(0, 128, finish, 0)


def steps_kernel(
    first, pressure, courant, snapshots, later, out_pressure, out_previous, image,
    field_a, field_b, zterm, dz, ysend, yrecv_a, yrecv_b, hsend, hrecv,
):
    a, b = lax.axis_index("gx"), lax.axis_index("gy")
    sem = pltpu.get_barrier_semaphore()
    near = (("gy", b - 1, b > 0), ("gy", b + 1, b < NY - 1), ("gx", a - 1, a > 0), ("gx", a + 1, a < NX - 1))
    for axis, device, there in near:
        @pl.when(there)
        def _():
            pl.semaphore_signal(sem, inc=1, device_id={axis: device}, device_id_type=MESH)

    def load(x, _):
        for half in range(2):
            lanes = pl.ds(half * 128, 128)
            now = first[x, half]
            field_a[x + 4, half, pl.ds(8, 32), :] = now
            field_b[x + 4, half, pl.ds(8, 32), :] = pressure[x, :, lanes]
            image[x, :, lanes] = snapshots[0, x, :, lanes] * now
        return 0

    lax.fori_loop(0, 32, load, 0)
    clear_edges(field_a, [yrecv_a])
    clear_edges(field_b, [yrecv_b])
    dz[...] = z_matrix()
    pl.semaphore_wait(sem, sum(there.astype(jnp.int32) for _, _, there in near))

    fields, yrecvs = (field_a, field_b), (yrecv_a, yrecv_b)
    halo = Halo(field_a, ysend, yrecv_a, (hsend, hrecv), 0)
    halo.start_y()
    halo.start_x()
    for t in range(1, STEPS):
        now, nxt = fields[(t - 1) % 2], fields[t % 2]
        last = t == STEPS - 1

        def update(x, half, tile):
            lanes, rows, inner = pl.ds(half * 128, 128), pl.ds(tile * 8, 8), pl.ds(8 + tile * 8, 8)
            centre = now[x + 4, half, inner, :]
            out = 2.0 * centre - nxt[x + 4, half, inner, :]
            out = out + courant[x, rows, lanes] * laplacian(now, zterm, x, half, tile)
            out = out + later[t - 1, x, half, rows, :]
            image[x, rows, lanes] = image[x, rows, lanes] + snapshots[t, x, rows, lanes] * out
            if last:
                out_pressure[x, rows, lanes] = out
                out_previous[x, rows, lanes] = centre
            else:
                nxt[x + 4, half, inner, :] = out

        def region(low, high, tiles):
            def body(x, _):
                for half in range(2):
                    for tile in tiles:
                        update(x, half, tile)
                return 0

            lax.fori_loop(low, high, body, 0)

        z_terms(now, dz, zterm)
        region(4, 28, (1, 2))
        halo.wait()
        region(0, 32, (0, 3))
        if not last:
            halo = Halo(nxt, ysend, yrecvs[t % 2], (hsend, hrecv), t)
            halo.start_y()
        region(0, 4, (1, 2))
        region(28, 32, (1, 2))
        if not last:
            halo.start_x()


def local(pressure, previous, courant, snapshots, traces, cell_offsets, live_counts):
    f32 = jnp.float32
    vmem, anywhere = pl.BlockSpec(memory_space=pltpu.VMEM), pl.BlockSpec(memory_space=pl.ANY)
    slot = jnp.arange(128, dtype=jnp.int32)
    live = slot[None, :] < live_counts.reshape(128, 1)
    offsets = cell_offsets.reshape(128, 128)
    margin = 8 - 4 * lax.rem(lax.axis_index("gy"), 2)
    codes = (((offsets >> 7) * 4 + margin) << 8) | (offsets & 127) | jnp.where(live, 0, 128)
    dma, halo_shape = pltpu.SemaphoreType.DMA, (2, 32, 2, 4, 128)
    values, codes, hom = pl.pallas_call(
        deliver_kernel,
        out_shape=(
            jax.ShapeDtypeStruct((NX, NY, 4, 128), f32),
            jax.ShapeDtypeStruct((NX, NY, 1, 128), jnp.int32),
            jax.ShapeDtypeStruct(BLOCK, f32),
        ),
        in_specs=[anywhere, anywhere, vmem, vmem, vmem],
        out_specs=(anywhere, anywhere, vmem),
        scratch_shapes=[
            pltpu.VMEM((NY, NX, 4, 128), f32),
            pltpu.VMEM((NY, NX, 1, 128), jnp.int32),
            pltpu.VMEM(FIELD, f32),
            pltpu.VMEM(BLOCK, f32),
            pltpu.VMEM((256, 256), f32),
            pltpu.VMEM(halo_shape, f32),
            pltpu.VMEM(halo_shape, f32),
            dma((4,)),
            dma((NY - 1, 2)),
            dma((NY - 1, 2)),
            dma((NX - 1, 2)),
            dma((NX - 1, 2)),
            dma((1, 4)),
            dma((1, 4)),
        ],
        compiler_params=pltpu.CompilerParams(
            collective_id=0, has_side_effects=True, vmem_limit_bytes=24 * 2**20
        ),
        name="deliver",
    )(traces.reshape(NX, NY, 4, 128), codes.reshape(NX, NY, 1, 128), pressure, previous, courant)
    first, later = pl.pallas_call(
        scatter_kernel,
        out_shape=(jax.ShapeDtypeStruct(BLOCK, f32), jax.ShapeDtypeStruct((3,) + BLOCK, f32)),
        in_specs=[pl.BlockSpec(memory_space=pltpu.SMEM), vmem, vmem],
        out_specs=(vmem, vmem),
        scratch_shapes=[pltpu.VMEM((ROWS, 128), f32)] * K,
        compiler_params=pltpu.CompilerParams(vmem_limit_bytes=40 * 2**20),
        name="scatter",
    )(codes.reshape(128, 128), values.reshape(128, 4, 128), hom)
    block = jax.ShapeDtypeStruct((32, 32, 256), f32)
    return pl.pallas_call(
        steps_kernel,
        out_shape=(block, block, block),
        in_specs=[vmem] * 5,
        out_specs=(vmem, vmem, vmem),
        scratch_shapes=[
            pltpu.VMEM(FIELD, f32),
            pltpu.VMEM(FIELD, f32),
            pltpu.VMEM(BLOCK, f32),
            pltpu.VMEM((256, 256), f32),
            pltpu.VMEM(halo_shape, f32),
            pltpu.VMEM(halo_shape, f32),
            pltpu.VMEM(halo_shape, f32),
            dma((3, 4)),
            dma((3, 4)),
        ],
        compiler_params=pltpu.CompilerParams(
            collective_id=1, has_side_effects=True, vmem_limit_bytes=40 * 2**20
        ),
        name="steps",
    )(first, pressure, courant, snapshots, later)


def solution(mesh):
    field = P("gx", "gy", None)
    return jax.shard_map(
        local,
        mesh=mesh,
        in_specs=(
            field,
            field,
            field,
            P(None, "gx", "gy", None),
            P(("gx", "gy"), None, None, None),
            P(("gx", "gy"), None, None),
            P(("gx", "gy"), None),
        ),
        out_specs=(field, field, field),
        check_vma=False,
    )
```

time: 539 us -> 88 us (0.16)
  other arithmetic: 392 us -> 2.39 us
  starting transfers between devices: 114 us -> 0 us
  Pallas kernels: 0 us -> 74.3 us
  local copies, waits for them, and re-layouts: 26.4 us -> 10.3 us
    scatter-add x4 -> x0, other arithmetic: 353 us -> none  [local(): nxt = nxt.reshape(-1).at[arrived_cells].add(values).reshape(pressure.shape)]
    pallas_call x0 -> x3, Pallas kernels: none -> 74.3 us  [the longest x1 27.6 us: local(): pl.pallas_call(scatter_kernel, out_shape=(jax.ShapeDtypeStruct(BLOCK, f32...]
    all_to_all x5 -> x0, starting transfers between devices: 66.4 us -> none  [the longest x4 55.9 us: local(): lax.all_to_all(masked[:, :, step, :], ('gx', 'gy'), split_axis=1, concat_...]
    ppermute x16 -> x0, starting transfers between devices: 47.6 us -> none  [the longest x8 31.3 us: extended(): lax.ppermute(lax.slice_in_dim(block, block.shape[dim] - width, None, axis...]
    add x5 -> x0, other arithmetic: 25.8 us -> none  [the longest x4 21.1 us: local(): 2.0 * pressure - previous]
    concatenate x4 -> x0, other arithmetic: 10.5 us -> none  [extended(): block = jnp.concatenate([low, block, high], axis=dim)]
    slice x15 -> x0, local copies, waits for them, and re-layouts: 8.38 us -> none  [the longest x11 6.23 us: extended(): lax.slice_in_dim(block, 0, width, axis=dim)]
    unnamed x46 -> x18, local copies, waits for them, and re-layouts: 13.5 us -> 10.2 us
  transfers between devices with their start and end apart: 21 -> 0, of which waited for: 2 -> 0; matrix products, arithmetic and copies ran while one was open for 9% -> 0% of each run, Pallas kernels for 0% -> 0%
where the time goes in v1:
time: 88 us; the launch traced here: 87.7 us
  Pallas kernels  74.3 us (84%)
  local copies, waits for them, and re-layouts  10.3 us (12%)
  other arithmetic  2.39 us (3%)
    pallas_call x1, Pallas kernels, local(): pl.pallas_call(scatter_kernel, out_shape=(jax.ShapeDtypeStruct(BLOCK, f32...  27.6 us
    pallas_call x1, Pallas kernels, local(): pl.pallas_call(steps_kernel, out_shape=(block, block, block), in_specs=[v...  23.7 us
    pallas_call x1, Pallas kernels, local(): pl.pallas_call(deliver_kernel, out_shape=(jax.ShapeDtypeStruct((NX, NY, 4...  23 us
    unnamed x18, local copies, waits for them, and re-layouts  10.2 us

profile of v1, /device:TPU:6, one launch (start us, length us, event | category | flops | bytes accessed | tf_op | source)
XLA Modules:
  0.0 87.7 jit_solution(14405743492921428077)
XLA Ops:
  0.6 0.5 broadcast.75
  1.1 1.3 %reduce.3 = s32[128]{0:T(128)S(1)} reduce(s32[1,128]{1,0:T(1,128)} %param.13, s32[]{:T(128)} %broadcast.75), dimensions={0}, to_apply=%param.13.reduce_sub_computation.3 | reduce | bytes 1028 | tf_op args[6]
  2.5 0.1 lt.23
  2.5 0.9 and_or_fusion
  3.4 0.2 fusion.codes
  3.6 0.0 copy-start
  3.6 1.2 %copy-done = f32[32,32,256]{2,1,0:T(8,128)S(1)} copy-done((f32[32,32,256]{2,1,0:T(8,128)S(1)}, f32[32,32,256]{2,1,0:T(8,128)}, u32[]{:S(2)}) %copy-start) | copy-done | bytes 1048600
  4.9 0.0 copy-start.2
  4.9 1.2 %copy-done.2 = f32[32,32,256]{2,1,0:T(8,128)S(1)} copy-done((f32[32,32,256]{2,1,0:T(8,128)S(1)}, f32[32,32,256]{2,1,0:T(8,128)}, u32[]{:S(2)}) %copy-start.2) | copy-done | bytes 1048600
  6.1 0.0 copy-start.5
  6.1 1.2 %copy-done.5 = f32[32,32,256]{2,1,0:T(8,128)S(1)} copy-done((f32[32,32,256]{2,1,0:T(8,128)S(1)}, f32[32,32,256]{2,1,0:T(8,128)}, u32[]{:S(2)}) %copy-start.5) | copy-done | bytes 1048600
  7.3 0.0 copy-start.6
  7.3 0.9 %copy-done.6 = f32[1,128,4,128]{3,2,1,0:T(4,128)S(1)} copy-done((f32[1,128,4,128]{3,2,1,0:T(4,128)S(1)}, f32[1,128,4,128]{3,2,1,0:T(4,128)}, u32[]{:S(2)}) %copy-start.6) | copy-done | bytes 262168
  8.3 0.0 copy-start.1
  8.3 0.0 copy-start.3
  8.3 23.0 %deliver.1 = (f32[16,8,4,128]{3,2,1,0:T(4,128)S(1)}, s32[16,8,1,128]{3,2,1,0:T(1,128)S(1)}, f32[32,2,32,128]{3,2,1,0:T(8,128)S(1)}) custom-call(f32[16,8,4,128]{3,2,1,0:T(4,128)S(1)} %bitcast.5, s32[16,8,1,128]{3,2,1,0:T(1,128)S(1)} %fusion.codes, f32[32,32,256]{2,1,0:T(8,128)S(1)} %copy-done, f32[32,32,256]{2,1,0:T(8,128)S(1)} %copy-done.5, ...), custom_call_target="tpu_custom_call" | custom-call | tf_op jit(solution)/shard_map/deliver/pallas_call | solution.py:352
  31.2 27.6 %scatter.1 = (f32[32,2,32,128]{3,2,1,0:T(8,128)S(1)}, f32[3,32,2,32,128]{4,3,2,1,0:T(8,128)S(1)}) custom-call(s32[128,128]{1,0:T(8,128)S(1)} %bitcast.6, f32[128,4,128]{2,1,0:T(4,128)S(1)} %bitcast.4, f32[32,2,32,128]{3,2,1,0:T(8,128)S(1)} %get-tuple-element.10.hom), custom_call_target="tpu_custom_call" | custom-call | tf_op jit(solution)/shard_map/scatter/pallas_call | solution.py:382
  58.9 0.0 copy-done.1
  58.9 0.0 copy-done.3
  58.9 0.0 copy-start.4
  58.9 2.2 %copy-done.4 = f32[4,32,32,256]{3,2,1,0:T(8,128)S(1)} copy-done((f32[4,32,32,256]{3,2,1,0:T(8,128)S(1)}, f32[4,32,32,256]{3,2,1,0:T(8,128)}, u32[]{:S(2)}) %copy-start.4) | copy-done | bytes 4194328
  61.1 23.7 %steps.1 = (f32[32,32,256]{2,1,0:T(8,128)S(1)}, f32[32,32,256]{2,1,0:T(8,128)S(1)}, f32[32,32,256]{2,1,0:T(8,128)S(1)}) custom-call(f32[32,2,32,128]{3,2,1,0:T(8,128)S(1)} %get-tuple-element.11.first, f32[32,32,256]{2,1,0:T(8,128)S(1)} %copy-done.1, f32[32,32,256]{2,1,0:T(8,128)S(1)} %copy-done.3, f32[4,32,32,256]{3,2,1,0:T(8,128)S(1)} %copy-done.4, ...), custom_call_target="tpu_custom_call" | custom-call | tf_op jit(solution)/shard_map/steps/pallas_call | solution.py:392
  84.8 1.0 %copy.13 = f32[32,32,256]{2,1,0:T(8,128)} copy(f32[32,32,256]{2,1,0:T(8,128)S(1)} %get-tuple-element.16) | data formatting | bytes 2097152
  85.7 1.0 %copy.14 = f32[32,32,256]{2,1,0:T(8,128)} copy(f32[32,32,256]{2,1,0:T(8,128)S(1)} %get-tuple-element.17) | data formatting | bytes 2097152
  86.7 1.0 %copy.15 = f32[32,32,256]{2,1,0:T(8,128)} copy(f32[32,32,256]{2,1,0:T(8,128)S(1)} %get-tuple-element.18) | data formatting | bytes 2097152
Async XLA Ops:
  3.6 1.2 %copy-start = (f32[32,32,256]{2,1,0:T(8,128)S(1)}, f32[32,32,256]{2,1,0:T(8,128)}, u32[]{:S(2)}) copy-start(f32[32,32,256]{2,1,0:T(8,128)} %pressure.3) | copy-start | bytes 3145732
  4.9 1.2 %copy-start.2 = (f32[32,32,256]{2,1,0:T(8,128)S(1)}, f32[32,32,256]{2,1,0:T(8,128)}, u32[]{:S(2)}) copy-start(f32[32,32,256]{2,1,0:T(8,128)} %courant.3) | copy-start | bytes 3145732
  6.1 1.2 %copy-start.5 = (f32[32,32,256]{2,1,0:T(8,128)S(1)}, f32[32,32,256]{2,1,0:T(8,128)}, u32[]{:S(2)}) copy-start(f32[32,32,256]{2,1,0:T(8,128)} %previous.1) | copy-start | bytes 3145732
  7.3 0.9 %copy-start.6 = (f32[1,128,4,128]{3,2,1,0:T(4,128)S(1)}, f32[1,128,4,128]{3,2,1,0:T(4,128)}, u32[]{:S(2)}) copy-start(f32[1,128,4,128]{3,2,1,0:T(4,128)} %param.11) | copy-start | bytes 786436
  8.3 50.6 %copy-start.1 = (f32[32,32,256]{2,1,0:T(8,128)S(1)}, f32[32,32,256]{2,1,0:T(8,128)}, u32[]{:S(2)}) copy-start(f32[32,32,256]{2,1,0:T(8,128)} %pressure.3) | copy-start | bytes 3145732
  8.3 50.6 %copy-start.3 = (f32[32,32,256]{2,1,0:T(8,128)S(1)}, f32[32,32,256]{2,1,0:T(8,128)}, u32[]{:S(2)}) copy-start(f32[32,32,256]{2,1,0:T(8,128)} %courant.3) | copy-start | bytes 3145732
  58.9 2.2 %copy-start.4 = (f32[4,32,32,256]{3,2,1,0:T(8,128)S(1)}, f32[4,32,32,256]{3,2,1,0:T(8,128)}, u32[]{:S(2)}) copy-start(f32[4,32,32,256]{3,2,1,0:T(8,128)} %snapshots.1) | copy-start | bytes 12582916

commit v2 on v1

--- a/solution.py
+++ b/solution.py
@@ -136,23 +136,35 @@
 
 
 def deliver_kernel(
-    traces, codes, pressure, previous, courant, values_out, codes_out, hom,
-    mid_values, mid_codes, field, zterm, dz, ysend, yrecv,
-    local_sem, send1, recv1, send2, recv2, hsend, hrecv,
+    traces, offsets_hbm, live_hbm, pressure_hbm, previous_hbm, courant_hbm,
+    values_out, codes_out, hom, pressure, courant,
+    offsets, live, codes, previous, mid_values, mid_codes, field, zterm, dz, ysend, yrecv,
+    load_sem, local_sem, send1, recv1, send2, recv2, hsend, hrecv,
 ):
     a, b = lax.axis_index("gx"), lax.axis_index("gy")
+    loads = [
+        pltpu.make_async_copy(src, dst, load_sem.at[i])
+        for i, (src, dst) in enumerate((
+            (offsets_hbm, offsets), (live_hbm, live), (pressure_hbm, pressure),
+            (previous_hbm, previous), (courant_hbm, courant),
+        ))
+    ]
+    for copy in loads:
+        copy.start()
     sem = pltpu.get_barrier_semaphore()
     peers = [("gy", lax.rem(b + o, NY)) for o in range(1, NY)]
     peers += [("gx", lax.rem(a + o, NX)) for o in range(1, NX)]
     for axis, device in peers:
         pl.semaphore_signal(sem, inc=1, device_id={axis: device}, device_id_type=MESH)
 
-    def load(x, _):
-        for half in range(2):
-            field[x + 4, half, pl.ds(8, 32), :] = pressure[x, :, half * 128 : half * 128 + 128]
-        return 0
-
-    lax.fori_loop(0, 32, load, 0)
+    loads[0].wait()
+    loads[1].wait()
+    lane = lax.broadcasted_iota(jnp.int32, (128, 128), 1)
+    counts = jnp.broadcast_to(live[...].astype(jnp.float32), (128, 128)).T.astype(jnp.int32)
+    cells = offsets[...]
+    margin = 8 - 4 * lax.rem(b, 2)
+    code = (((cells >> 7) * 4 + margin) << 8) | (cells & 127) | jnp.where(lane < counts, 0, 128)
+    codes[...] = code.reshape(NX, NY, 1, 128)
     clear_edges(field, [yrecv])
     pl.semaphore_wait(sem, len(peers))
 
@@ -173,6 +185,14 @@
         copy.start()
     for copy in own1:
         copy.start()
+    loads[2].wait()
+
+    def load(x, _):
+        for half in range(2):
+            field[x + 4, half, pl.ds(8, 32), :] = pressure[x, :, half * 128 : half * 128 + 128]
+        return 0
+
+    lax.fori_loop(0, 32, load, 0)
     halo = Halo(field, ysend, yrecv, (hsend, hrecv), 0)
     halo.start_y()
     halo.start_x()
@@ -204,6 +224,8 @@
         copy.start()
 
     halo.wait()
+    loads[3].wait()
+    loads[4].wait()
 
     def step(x, _):
         for half in range(2):
@@ -271,8 +293,8 @@
 
 
 def steps_kernel(
-    first, pressure, courant, snapshots, later, out_pressure, out_previous, image,
-    field_a, field_b, zterm, dz, ysend, yrecv_a, yrecv_b, hsend, hrecv,
+    first, pressure, courant, snapshots, later, field_a, field_b, zterm, image,
+    dz, ysend, yrecv_a, yrecv_b, hsend, hrecv,
 ):
     a, b = lax.axis_index("gx"), lax.axis_index("gy")
     sem = pltpu.get_barrier_semaphore()
@@ -284,26 +306,30 @@
 
     def load(x, _):
         for half in range(2):
-            lanes = pl.ds(half * 128, 128)
-            now = first[x, half]
-            field_a[x + 4, half, pl.ds(8, 32), :] = now
-            field_b[x + 4, half, pl.ds(8, 32), :] = pressure[x, :, lanes]
-            image[x, :, lanes] = snapshots[0, x, :, lanes] * now
+            field_a[x + 4, half, pl.ds(8, 32), :] = first[x, half]
         return 0
 
     lax.fori_loop(0, 32, load, 0)
     clear_edges(field_a, [yrecv_a])
     clear_edges(field_b, [yrecv_b])
-    dz[...] = z_matrix()
     pl.semaphore_wait(sem, sum(there.astype(jnp.int32) for _, _, there in near))
 
     fields, yrecvs = (field_a, field_b), (yrecv_a, yrecv_b)
     halo = Halo(field_a, ysend, yrecv_a, (hsend, hrecv), 0)
     halo.start_y()
     halo.start_x()
-    for t in range(1, STEPS):
+    dz[...] = z_matrix()
+
+    def load_previous(x, _):
+        for half in range(2):
+            lanes = pl.ds(half * 128, 128)
+            field_b[x + 4, half, pl.ds(8, 32), :] = pressure[x, :, lanes]
+            image[x, :, lanes] = snapshots[0, x, :, lanes] * first[x, half]
+        return 0
+
+    lax.fori_loop(0, 32, load_previous, 0)
+    for t in range(1, STEPS - 1):
         now, nxt = fields[(t - 1) % 2], fields[t % 2]
-        last = t == STEPS - 1
 
         def update(x, half, tile):
             lanes, rows, inner = pl.ds(half * 128, 128), pl.ds(tile * 8, 8), pl.ds(8 + tile * 8, 8)
@@ -312,11 +338,7 @@
             out = out + courant[x, rows, lanes] * laplacian(now, zterm, x, half, tile)
             out = out + later[t - 1, x, half, rows, :]
             image[x, rows, lanes] = image[x, rows, lanes] + snapshots[t, x, rows, lanes] * out
-            if last:
-                out_pressure[x, rows, lanes] = out
-                out_previous[x, rows, lanes] = centre
-            else:
-                nxt[x + 4, half, inner, :] = out
+            nxt[x + 4, half, inner, :] = out
 
         def region(low, high, tiles):
             def body(x, _):
@@ -331,34 +353,74 @@
         region(4, 28, (1, 2))
         halo.wait()
         region(0, 32, (0, 3))
-        if not last:
-            halo = Halo(nxt, ysend, yrecvs[t % 2], (hsend, hrecv), t)
-            halo.start_y()
+        halo = Halo(nxt, ysend, yrecvs[t % 2], (hsend, hrecv), t)
+        halo.start_y()
         region(0, 4, (1, 2))
         region(28, 32, (1, 2))
-        if not last:
-            halo.start_x()
+        halo.start_x()
+    z_terms(fields[STEPS % 2], dz, zterm)
+    halo.wait()
+
+
+def last_kernel(
+    now, before, zterm, image_in, later, courant, snapshots, pressure_hbm, previous_hbm, image_hbm,
+    pressure, image, out_sem,
+):
+    stores = [
+        pltpu.make_async_copy(
+            now.at[pl.ds(4, 32), half, pl.ds(8, 32), :],
+            previous_hbm.at[:, :, pl.ds(half * 128, 128)], out_sem.at[half],
+        )
+        for half in range(2)
+    ]
+    for copy in stores:
+        copy.start()
+    for part in range(4):
+        def body(x, _):
+            for half in range(2):
+                for tile in range(4):
+                    lanes, rows, inner = pl.ds(half * 128, 128), pl.ds(tile * 8, 8), pl.ds(8 + tile * 8, 8)
+                    out = 2.0 * now[x + 4, half, inner, :] - before[x + 4, half, inner, :]
+                    out = out + courant[x, rows, lanes] * laplacian(now, zterm, x, half, tile)
+                    out = out + later[STEPS - 2, x, half, rows, :]
+                    image[x, rows, lanes] = image_in[x, rows, lanes] + snapshots[STEPS - 1, x, rows, lanes] * out
+                    pressure[x, rows, lanes] = out
+            return 0
+
+        lax.fori_loop(part * 8, part * 8 + 8, body, 0)
+        xs = pl.ds(part * 8, 8)
+        stores += [
+            pltpu.make_async_copy(pressure.at[xs], pressure_hbm.at[xs], out_sem.at[2 + 2 * part]),
+            pltpu.make_async_copy(image.at[xs], image_hbm.at[xs], out_sem.at[3 + 2 * part]),
+        ]
+        stores[-2].start()
+        stores[-1].start()
+    for copy in stores:
+        copy.wait()
 
 
 def local(pressure, previous, courant, snapshots, traces, cell_offsets, live_counts):
     f32 = jnp.float32
     vmem, anywhere = pl.BlockSpec(memory_space=pltpu.VMEM), pl.BlockSpec(memory_space=pl.ANY)
-    slot = jnp.arange(128, dtype=jnp.int32)
-    live = slot[None, :] < live_counts.reshape(128, 1)
-    offsets = cell_offsets.reshape(128, 128)
-    margin = 8 - 4 * lax.rem(lax.axis_index("gy"), 2)
-    codes = (((offsets >> 7) * 4 + margin) << 8) | (offsets & 127) | jnp.where(live, 0, 128)
+    hbm = pl.BlockSpec(memory_space=pltpu.HBM)
     dma, halo_shape = pltpu.SemaphoreType.DMA, (2, 32, 2, 4, 128)
-    values, codes, hom = pl.pallas_call(
+    block, wide = jax.ShapeDtypeStruct((32, 32, 256), f32), jax.ShapeDtypeStruct(FIELD, f32)
+    values, codes, hom, pressure, courant = pl.pallas_call(
         deliver_kernel,
         out_shape=(
             jax.ShapeDtypeStruct((NX, NY, 4, 128), f32),
             jax.ShapeDtypeStruct((NX, NY, 1, 128), jnp.int32),
             jax.ShapeDtypeStruct(BLOCK, f32),
+            block,
+            block,
         ),
-        in_specs=[anywhere, anywhere, vmem, vmem, vmem],
-        out_specs=(anywhere, anywhere, vmem),
+        in_specs=[hbm] * 6,
+        out_specs=(anywhere, anywhere, vmem, vmem, vmem),
         scratch_shapes=[
+            pltpu.VMEM((128, 128), jnp.int32),
+            pltpu.VMEM((1, 128), jnp.int32),
+            pltpu.VMEM((NX, NY, 1, 128), jnp.int32),
+            pltpu.VMEM((32, 32, 256), f32),
             pltpu.VMEM((NY, NX, 4, 128), f32),
             pltpu.VMEM((NY, NX, 1, 128), jnp.int32),
             pltpu.VMEM(FIELD, f32),
@@ -366,6 +428,7 @@
             pltpu.VMEM((256, 256), f32),
             pltpu.VMEM(halo_shape, f32),
             pltpu.VMEM(halo_shape, f32),
+            dma((5,)),
             dma((4,)),
             dma((NY - 1, 2)),
             dma((NY - 1, 2)),
@@ -375,29 +438,28 @@
             dma((1, 4)),
         ],
         compiler_params=pltpu.CompilerParams(
-            collective_id=0, has_side_effects=True, vmem_limit_bytes=24 * 2**20
+            collective_id=0, has_side_effects=True, vmem_limit_bytes=51300 * 1024
         ),
         name="deliver",
-    )(traces.reshape(NX, NY, 4, 128), codes.reshape(NX, NY, 1, 128), pressure, previous, courant)
+    )(
+        traces.reshape(NX, NY, 4, 128), cell_offsets.reshape(128, 128), live_counts,
+        pressure, previous, courant,
+    )
     first, later = pl.pallas_call(
         scatter_kernel,
         out_shape=(jax.ShapeDtypeStruct(BLOCK, f32), jax.ShapeDtypeStruct((3,) + BLOCK, f32)),
         in_specs=[pl.BlockSpec(memory_space=pltpu.SMEM), vmem, vmem],
         out_specs=(vmem, vmem),
         scratch_shapes=[pltpu.VMEM((ROWS, 128), f32)] * K,
-        compiler_params=pltpu.CompilerParams(vmem_limit_bytes=40 * 2**20),
+        compiler_params=pltpu.CompilerParams(vmem_limit_bytes=38000 * 1024),
         name="scatter",
     )(codes.reshape(128, 128), values.reshape(128, 4, 128), hom)
-    block = jax.ShapeDtypeStruct((32, 32, 256), f32)
-    return pl.pallas_call(
+    now, before, zterm, image = pl.pallas_call(
         steps_kernel,
-        out_shape=(block, block, block),
+        out_shape=(wide, wide, jax.ShapeDtypeStruct(BLOCK, f32), block),
         in_specs=[vmem] * 5,
-        out_specs=(vmem, vmem, vmem),
+        out_specs=(vmem,) * 4,
         scratch_shapes=[
-            pltpu.VMEM(FIELD, f32),
-            pltpu.VMEM(FIELD, f32),
-            pltpu.VMEM(BLOCK, f32),
             pltpu.VMEM((256, 256), f32),
             pltpu.VMEM(halo_shape, f32),
             pltpu.VMEM(halo_shape, f32),
@@ -406,10 +468,19 @@
             dma((3, 4)),
         ],
         compiler_params=pltpu.CompilerParams(
-            collective_id=1, has_side_effects=True, vmem_limit_bytes=40 * 2**20
+            collective_id=1, has_side_effects=True, vmem_limit_bytes=24000 * 1024
         ),
         name="steps",
     )(first, pressure, courant, snapshots, later)
+    return pl.pallas_call(
+        last_kernel,
+        out_shape=(block, block, block),
+        in_specs=[vmem] * 7,
+        out_specs=(hbm,) * 3,
+        scratch_shapes=[pltpu.VMEM((32, 32, 256), f32)] * 2 + [dma((10,))],
+        compiler_params=pltpu.CompilerParams(vmem_limit_bytes=24000 * 1024),
+        name="last",
+    )(now, before, zterm, image, later, courant, snapshots)
 
 
 def solution(mesh):

time: 88 us -> 79.7 us (0.906)
  local copies, waits for them, and re-layouts: 10.3 us -> 2.82 us
  other arithmetic: 2.39 us -> 0 us
  Pallas kernels: 74.3 us -> 76.1 us
    unnamed x18 -> x8, local copies, waits for them, and re-layouts: 10.2 us -> 2.82 us
    pallas_call x1 -> x2, Pallas kernels: 23.7 us -> 25.5 us  [the longest x1 22.9 us: local(): pl.pallas_call(steps_kernel, out_shape=(wide, wide, jax.ShapeDtypeStruct(...]
    unnamed x1 -> x0, other arithmetic: 1.32 us -> none
    or x2 -> x0, other arithmetic: 1.07 us -> none  [local(): (offsets >> 7) * 4 + margin << 8 | offsets & 127 | jnp.where(live, 0, 128)]
where the time goes in v2:
time: 79.7 us; the launch traced here: 79.6 us
  Pallas kernels  76.1 us (95%)
  local copies, waits for them, and re-layouts  2.82 us (4%)
    pallas_call x1, Pallas kernels, local(): pl.pallas_call(scatter_kernel, out_shape=(jax.ShapeDtypeStruct(BLOCK, f32...  27.6 us
    pallas_call x1, Pallas kernels, local(): pl.pallas_call(deliver_kernel, out_shape=(jax.ShapeDtypeStruct((NX, NY, 4...  23 us
    pallas_call x1, Pallas kernels, local(): pl.pallas_call(steps_kernel, out_shape=(wide, wide, jax.ShapeDtypeStruct(...  22.9 us
    unnamed x8, local copies, waits for them, and re-layouts  2.82 us
    pallas_call x1, Pallas kernels, local(): pl.pallas_call(last_kernel, out_shape=(block, block, block), in_specs=[vm...  2.64 us

profile of v2, /device:TPU:6, one launch (start us, length us, event | category | flops | bytes accessed | tf_op | source)
XLA Modules:
  0.0 79.6 jit_solution(17632618757512751013)
XLA Ops:
  0.6 0.0 copy-start
  0.6 0.0 copy-start.1
  0.7 1.1 %copy-done.1 = f32[1,128,4,128]{3,2,1,0:T(4,128)S(1)} copy-done((f32[1,128,4,128]{3,2,1,0:T(4,128)S(1)}, f32[1,128,4,128]{3,2,1,0:T(4,128)}, u32[]{:S(2)}) %copy-start.1) | copy-done | bytes 262168
  1.7 0.0 copy-start.2
  1.7 1.1 %copy-done.2 = s32[1,128,128]{2,1,0:T(8,128)S(1)} copy-done((s32[1,128,128]{2,1,0:T(8,128)S(1)}, s32[1,128,128]{2,1,0:T(8,128)}, u32[]{:S(2)}) %copy-start.2) | copy-done | bytes 65560
  2.8 0.0 copy-start.3
  2.8 0.7 copy-done.3
  3.5 23.0 %deliver.1 = (f32[16,8,4,128]{3,2,1,0:T(4,128)S(1)}, s32[16,8,1,128]{3,2,1,0:T(1,128)S(1)}, f32[32,2,32,128]{3,2,1,0:T(8,128)S(1)}, f32[32,32,256]{2,1,0:T(8,128)S(1)}, f32[32,32,256]{2,1,0:T(8,128)S(1)}) custom-call(f32[16,8,4,128]{3,2,1,0:T(4,128)S(1)} %bitcast.4, s32[128,128]{1,0:T(8,128)S(1)} %bitcast.6, s32[1,128]{1,0:T(1,128)S(1)} %copy-done.3, ...), custom_call_target="tpu_custom_call" | custom-call | tf_op jit(solution)/shard_map/deliver/pallas_call | solution.py:408
  26.4 27.6 %scatter.1 = (f32[32,2,32,128]{3,2,1,0:T(8,128)S(1)}, f32[3,32,2,32,128]{4,3,2,1,0:T(8,128)S(1)}) custom-call(s32[128,128]{1,0:T(8,128)S(1)} %bitcast.7, f32[128,4,128]{2,1,0:T(4,128)S(1)} %bitcast.5, f32[32,2,32,128]{3,2,1,0:T(8,128)S(1)} %get-tuple-element.16.hom), custom_call_target="tpu_custom_call" | custom-call | tf_op jit(solution)/shard_map/scatter/pallas_call | solution.py:448
  54.1 0.0 copy-done
  54.1 22.9 %steps.1 = (f32[40,2,48,128]{3,2,1,0:T(8,128)S(1)}, f32[40,2,48,128]{3,2,1,0:T(8,128)S(1)}, f32[32,2,32,128]{3,2,1,0:T(8,128)S(1)}, f32[32,32,256]{2,1,0:T(8,128)S(1)}) custom-call(f32[32,2,32,128]{3,2,1,0:T(8,128)S(1)} %get-tuple-element.17.first, f32[32,32,256]{2,1,0:T(8,128)S(1)} %get-tuple-element.18.pressure, ...), custom_call_target="tpu_custom_call" | custom-call | tf_op jit(solution)/shard_map/steps/pallas_call | solution.py:457
  76.9 2.6 %last.1 = (f32[32,32,256]{2,1,0:T(8,128)}, f32[32,32,256]{2,1,0:T(8,128)}, f32[32,32,256]{2,1,0:T(8,128)}) custom-call(f32[40,2,48,128]{3,2,1,0:T(8,128)S(1)} %get-tuple-element.21.now, f32[40,2,48,128]{3,2,1,0:T(8,128)S(1)} %get-tuple-element.22.before, f32[32,2,32,128]{3,2,1,0:T(8,128)S(1)} %get-tuple-element.23.zterm, ...), custom_call_target="tpu_custom_call" | custom-call | tf_op jit(solution)/shard_map/last/pallas_call | solution.py:475
Async XLA Ops:
  0.6 53.4 %copy-start = (f32[4,32,32,256]{3,2,1,0:T(8,128)S(1)}, f32[4,32,32,256]{3,2,1,0:T(8,128)}, u32[]{:S(2)}) copy-start(f32[4,32,32,256]{3,2,1,0:T(8,128)} %snapshots.3) | copy-start | bytes 12582916
  0.6 1.1 %copy-start.1 = (f32[1,128,4,128]{3,2,1,0:T(4,128)S(1)}, f32[1,128,4,128]{3,2,1,0:T(4,128)}, u32[]{:S(2)}) copy-start(f32[1,128,4,128]{3,2,1,0:T(4,128)} %param.11) | copy-start | bytes 786436
  1.7 1.1 %copy-start.2 = (s32[1,128,128]{2,1,0:T(8,128)S(1)}, s32[1,128,128]{2,1,0:T(8,128)}, u32[]{:S(2)}) copy-start(s32[1,128,128]{2,1,0:T(8,128)} %param.12) | copy-start | bytes 196612
  2.8 0.7 copy-start.3

commit v3 on v2

v3 whole, which is shorter than its diff:
```python
import functools

import jax
import jax.numpy as jnp
from jax import lax
from jax.experimental import pallas as pl
from jax.experimental.pallas import tpu as pltpu
from jax.sharding import PartitionSpec as P

STEPS = 4
COEFS = (-205.0 / 72.0, 8.0 / 5.0, -1.0 / 5.0, 8.0 / 315.0, -1.0 / 560.0)
NX, NY = 16, 8
K = 5
ROWS = 8192 + 16
MESH = pl.DeviceIdType.MESH
FIELD = (40, 2, 48, 128)
BLOCK = (32, 2, 32, 128)


def barrier(peers):
    sem = pltpu.get_barrier_semaphore()
    for axis, device in peers:
        pl.semaphore_signal(sem, inc=1, device_id={axis: device}, device_id_type=MESH)
    pl.semaphore_wait(sem, len(peers))


def z_matrix():
    row = lax.broadcasted_iota(jnp.int32, (256, 256), 0)
    col = lax.broadcasted_iota(jnp.int32, (256, 256), 1)
    apart = jnp.abs(row - col)
    matrix = jnp.where(apart == 0, 3.0 * COEFS[0], 0.0)
    for shift in range(1, 5):
        matrix = jnp.where(apart == shift, COEFS[shift], matrix)
    return matrix.astype(jnp.float32)


def z_terms(field, dz, zterm):
    def body(i, _):
        xs = pl.ds(4 + i * 8, 8)
        left = field[xs, 0, pl.ds(8, 32), :].reshape(256, 128)
        right = field[xs, 1, pl.ds(8, 32), :].reshape(256, 128)
        both = jnp.concatenate([left, right], axis=1)
        out = jnp.dot(both, dz[...], precision=lax.Precision.HIGHEST, preferred_element_type=jnp.float32)
        zterm[pl.ds(i * 8, 8), 0] = out[:, :128].reshape(8, 32, 128)
        zterm[pl.ds(i * 8, 8), 1] = out[:, 128:].reshape(8, 32, 128)
        return 0

    lax.fori_loop(0, 4, body, 0)


def laplacian(field, zterm, x, half, tile):
    rows = 8 + tile * 8
    total = zterm[x, half, pl.ds(tile * 8, 8), :]
    for shift in range(1, 5):
        pairs = field[x + 4 + shift, half, pl.ds(rows, 8), :] + field[x + 4 - shift, half, pl.ds(rows, 8), :]
        pairs = pairs + field[x + 4, half, pl.ds(rows + shift, 8), :]
        pairs = pairs + field[x + 4, half, pl.ds(rows - shift, 8), :]
        total = total + COEFS[shift] * pairs
    return total


class Halo:
    def __init__(self, field, landings, sems, index):
        a, b = lax.axis_index("gx"), lax.axis_index("gy")
        self.there = (b > 0, b < NY - 1, a > 0, a < NX - 1)
        self.come = (b < NY - 1, b > 0, a < NX - 1, a > 0)
        send, recv = sems
        xs, ys = pl.ds(4, 32), pl.ds(8, 32)
        faces = (
            (field.at[xs, :, pl.ds(8, 4), :], "gy", b - 1),
            (field.at[xs, :, pl.ds(36, 4), :], "gy", b + 1),
            (field.at[pl.ds(4, 4), :, ys, :], "gx", a - 1),
            (field.at[pl.ds(32, 4), :, ys, :], "gx", a + 1),
        )
        self.copies = [
            pltpu.make_async_remote_copy(
                src_ref=face, dst_ref=landing, send_sem=send.at[index, d], recv_sem=recv.at[index, d],
                device_id={axis: device}, device_id_type=MESH,
            )
            for d, ((face, axis, device), landing) in enumerate(zip(faces, landings))
        ]

    def start(self):
        for d in range(4):
            pl.when(self.there[d])(lambda: self.copies[d].start())

    def wait(self):
        for d in range(4):
            pl.when(self.come[d])(lambda: self.copies[d].wait_recv())
        for d in range(4):
            pl.when(self.there[d])(lambda: self.copies[d].wait_send())


def field_landings(field):
    xs, ys = pl.ds(4, 32), pl.ds(8, 32)
    return (
        field.at[xs, :, pl.ds(40, 4), :], field.at[xs, :, pl.ds(4, 4), :],
        field.at[pl.ds(36, 4), :, ys, :], field.at[pl.ds(0, 4), :, ys, :],
    )


def side_landings(xside, yside):
    return yside.at[1, :, :, pl.ds(8, 4), :], yside.at[0, :, :, pl.ds(4, 4), :], xside.at[1], xside.at[0]


def clear_field_edges(field):
    a, b = lax.axis_index("gx"), lax.axis_index("gy")
    for edge, low in ((a == 0, 0), (a == NX - 1, 36)):
        @pl.when(edge)
        def _():
            field[pl.ds(low, 4)] = jnp.zeros((4,) + FIELD[1:], jnp.float32)

    for edge, low in ((b == 0, 0), (b == NY - 1, 40)):
        @pl.when(edge)
        def _():
            field[:, :, pl.ds(low, 8), :] = jnp.zeros((40, 2, 8, 128), jnp.float32)


def clear_halo(field):
    for low in (0, 36):
        field[pl.ds(low, 4)] = jnp.zeros((4,) + FIELD[1:], jnp.float32)
    for low in (0, 40):
        field[pl.ds(4, 32), :, pl.ds(low, 8), :] = jnp.zeros((32, 2, 8, 128), jnp.float32)


def clear_sides(xside, yside):
    a, b = lax.axis_index("gx"), lax.axis_index("gy")
    rows = jnp.zeros((32, 2, 8, 128), jnp.float32)
    yside[0, :, :, pl.ds(8, 8), :] = rows
    yside[1, :, :, pl.ds(0, 8), :] = rows
    for edge, side, low in ((b == 0, 0, 0), (b == NY - 1, 1, 8)):
        @pl.when(edge)
        def _():
            yside[side, :, :, pl.ds(low, 8), :] = rows

    for edge, side in ((a == 0, 0), (a == NX - 1, 1)):
        @pl.when(edge)
        def _():
            xside[side] = jnp.zeros((4, 2, 32, 128), jnp.float32)


def y_face_terms(yside, x, half, tile):
    total = None
    for shift in range(1, 5):
        low = 8 - shift if tile == 0 else shift
        term = COEFS[shift] * yside[0 if tile == 0 else 1, x, half, pl.ds(low, 8), :]
        total = term if total is None else total + term
    return total


def x_face_terms(xside, side, layer, half, tile):
    total = None
    for shift in range(layer + 1, 5):
        there = 4 + layer - shift if side == 0 else shift - layer - 1
        term = COEFS[shift] * xside[side, there, half, pl.ds(tile * 8, 8), :]
        total = term if total is None else total + term
    return total


def deliver_kernel(
    traces, offsets_hbm, live_hbm, pressure_hbm, previous_hbm, courant_hbm,
    values_out, codes_out, hom, pressure, courant,
    offsets, live, codes, previous, mid_values0, mid_values1, mid_codes0, mid_codes1, field, zterm, dz,
    load_sem, local_sem, send1, recv1, send2, recv2, send3, recv3, send4, recv4, hsend, hrecv,
):
    a, b = lax.axis_index("gx"), lax.axis_index("gy")
    loads = [
        pltpu.make_async_copy(src, dst, load_sem.at[i])
        for i, (src, dst) in enumerate((
            (offsets_hbm, offsets), (live_hbm, live), (pressure_hbm, pressure),
            (previous_hbm, previous), (courant_hbm, courant),
        ))
    ]
    for copy in loads:
        copy.start()
    sem = pltpu.get_barrier_semaphore()
    peers = [("gy", lax.rem(b + o, NY)) for o in range(1, NY)]
    peers += [("gx", lax.rem(a + o, NX)) for o in range(1, NX)]
    for axis, device in peers:
        pl.semaphore_signal(sem, inc=1, device_id={axis: device}, device_id_type=MESH)

    loads[0].wait()
    loads[1].wait()
    lane = lax.broadcasted_iota(jnp.int32, (128, 128), 1)
    counts = jnp.broadcast_to(live[...].astype(jnp.float32), (128, 128)).T.astype(jnp.int32)
    cells = offsets[...]
    margin = 8 - 4 * lax.rem(b, 2)
    code = (((cells >> 7) * 4 + margin) << 8) | (cells & 127) | jnp.where(lane < counts, 0, 128)
    codes[...] = code.reshape(8, 2, NY, 1, 128)
    clear_field_edges(field)
    pl.semaphore_wait(sem, len(peers))

    core, pair = lax.rem(a, 2), a // 2
    both = ((traces, mid_values0, mid_values1, values_out), (codes, mid_codes0, mid_codes1, codes_out))

    def remote(src, dst, send, recv, device):
        return pltpu.make_async_remote_copy(
            src_ref=src, dst_ref=dst, send_sem=send, recv_sem=recv, device_id=device, device_id_type=MESH
        )

    gy_first, gx_first, gx_second, gy_second = [], [], [], []
    own_first, own_second, own_gx_first, own_gx_second = [], [], [], []
    for kind, (given, mid0, mid1, out) in enumerate(both):
        own_first.append(pltpu.make_async_copy(given.at[:, 0, b], mid0.at[b], local_sem.at[0, kind]))
        own_gx_first.append(pltpu.make_async_copy(given.at[pair, 1], mid1.at[a], local_sem.at[1, kind]))
        own_gx_second.append(pltpu.make_async_copy(mid0.at[:, pair], out.at[a], local_sem.at[2, kind]))
        own_second.append(pltpu.make_async_copy(mid1.at[:, b], out.at[:, b], local_sem.at[3, kind]))
    for o in range(1, NY):
        to = lax.rem(b + o, NY)
        for kind, (given, mid0, mid1, out) in enumerate(both):
            gy_first.append(remote(
                given.at[:, 0, to], mid0.at[b], send1.at[o - 1, kind], recv1.at[o - 1, kind], {"gy": to}
            ))
            gy_second.append(remote(
                mid1.at[:, to], out.at[:, b], send4.at[o - 1, kind], recv4.at[o - 1, kind], {"gy": to}
            ))
    for o in range(8):
        to = lax.rem(pair + o, 8)
        for kind, (given, mid0, mid1, out) in enumerate(both):
            gx_first.append(remote(
                given.at[to, 1], mid1.at[a], send2.at[o, kind], recv2.at[o, core, kind], {"gx": 2 * to + 1}
            ))
            gx_second.append(remote(
                mid0.at[:, to], out.at[a], send3.at[o, kind], recv3.at[o, core, kind], {"gx": 2 * to}
            ))

    def gx_arrived(recv, landing):
        for o in range(8):
            for sender in range(2):
                for kind in range(2):
                    def wait():
                        remote(
                            landing[kind], landing[kind], send2.at[o, kind], recv.at[o, sender, kind], {"gx": a}
                        ).wait_recv()

                    if o > 0:
                        wait()
                    else:
                        pl.when(core != sender)(wait)

    for n in range(16):
        if n < 14:
            gy_first[n].start()
        if n >= 2:
            gx_first[n].start()
    for copy in own_first:
        copy.start()

    @pl.when(core == 0)
    def _():
        gx_first[0].start()
        gx_first[1].start()

    @pl.when(core == 1)
    def _():
        own_gx_first[0].start()
        own_gx_first[1].start()

    loads[2].wait()

    def load(x, _):
        for half in range(2):
            field[x + 4, half, pl.ds(8, 32), :] = pressure[x, :, half * 128 : half * 128 + 128]
        return 0

    lax.fori_loop(0, 32, load, 0)
    halo = Halo(field, field_landings(field), (hsend, hrecv), 0)
    halo.start()

    dz[...] = z_matrix()
    z_terms(field, dz, zterm)

    for copy in own_first:
        copy.wait()
    for copy in gy_first:
        copy.wait_recv()
    for copy in gx_second[2:]:
        copy.start()

    @pl.when(core == 0)
    def _():
        own_gx_second[0].start()
        own_gx_second[1].start()

    @pl.when(core == 1)
    def _():
        gx_second[0].start()
        gx_second[1].start()
        own_gx_first[0].wait()
        own_gx_first[1].wait()
        gx_arrived(recv2, (mid_values1.at[0], mid_codes1.at[0]))
        for copy in gy_second:
            copy.start()
        for copy in own_second:
            copy.start()

    halo.wait()
    loads[3].wait()
    loads[4].wait()

    def step(x, _):
        for half in range(2):
            lanes = pl.ds(half * 128, 128)
            for tile in range(4):
                rows = pl.ds(tile * 8, 8)
                now = field[x + 4, half, pl.ds(8 + tile * 8, 8), :]
                out = 2.0 * now - previous[x, rows, lanes]
                hom[x, half, rows, :] = out + courant[x, rows, lanes] * laplacian(field, zterm, x, half, tile)
        return 0

    lax.fori_loop(0, 32, step, 0)

    for copy in gy_first:
        copy.wait_send()
    for copy in gx_first[2:]:
        copy.wait_send()
    for copy in gx_second[2:]:
        copy.wait_send()

    @pl.when(core == 0)
    def _():
        gx_first[0].wait_send()
        gx_first[1].wait_send()
        own_gx_second[0].wait()
        own_gx_second[1].wait()
        gx_arrived(recv3, (values_out.at[0], codes_out.at[0]))

    @pl.when(core == 1)
    def _():
        gx_second[0].wait_send()
        gx_second[1].wait_send()
        for copy in own_second:
            copy.wait()
        for copy in gy_second:
            copy.wait()


def scatter_kernel(codes, values, hom, first, later, *sums):
    zero = jnp.zeros((64, 128), jnp.float32)

    def clear(i, _):
        for total in sums:
            total[pl.ds(pl.multiple_of(i * 64, 64), 64), :] = zero
        return 0

    lax.fori_loop(0, 128, clear, 0)
    for total in sums:
        total[pl.ds(8192, 16), :] = jnp.zeros((16, 128), jnp.float32)
    sub = lax.broadcasted_iota(jnp.int32, (8, 128), 0)
    lane = lax.broadcasted_iota(jnp.int32, (8, 128), 1)
    place = (jnp.where(sub < 4, lane, -1), jnp.where(sub < 4, -1, lane))

    def body(s, _):
        both = jnp.concatenate([values[2 * s], values[2 * s + 1]], axis=0)
        for j in range(128):
            wide = jnp.broadcast_to(both[:, j : j + 1], (8, 128))
            for h in range(2):
                code = codes[2 * s + h, j]
                rows = pl.ds(code >> 8, 8)
                cell = jnp.full((8, 128), code, jnp.int32) & 255
                total = sums[(2 * j + h) % K]
                total[rows, :] = total[rows, :] + jnp.where(place[h] == cell, wide, 0.0)
        return 0

    lax.fori_loop(0, 64, body, 0)

    def finish(i, _):
        rows = pl.ds(pl.multiple_of(i * 64 + 8, 8), 64)
        total = sums[0][rows, :]
        for other in sums[1:]:
            total = total + other[rows, :]
        turned = jnp.swapaxes(total.reshape(8, 8, 128), 0, 1)
        x, ys = i // 4, pl.ds(pl.multiple_of(i % 4 * 8, 8), 8)
        for half in range(2):
            first[x, half, ys, :] = hom[x, half, ys, :] + turned[half * 4]
            for t in range(1, STEPS):
                later[t - 1, x, half, ys, :] = turned[half * 4 + t]
        return 0

    lax.fori_loop(0, 128, finish, 0)


def steps_kernel(
    first, pressure, courant, snapshots, later, field_a, out, image, xside_a, yside_a,
    field_b, zterm, dz, xside_b, yside_b, hsend, hrecv,
):
    a, b = lax.axis_index("gx"), lax.axis_index("gy")
    sem = pltpu.get_barrier_semaphore()
    near = (("gy", b - 1, b > 0), ("gy", b + 1, b < NY - 1), ("gx", a - 1, a > 0), ("gx", a + 1, a < NX - 1))
    for axis, device, there in near:
        @pl.when(there)
        def _():
            pl.semaphore_signal(sem, inc=1, device_id={axis: device}, device_id_type=MESH)

    def load(x, _):
        for half in range(2):
            field_a[x + 4, half, pl.ds(8, 32), :] = first[x, half]
        return 0

    lax.fori_loop(0, 32, load, 0)
    pl.semaphore_wait(sem, sum(there.astype(jnp.int32) for _, _, there in near))

    fields, sides = (field_a, field_b), ((xside_a, yside_a), (xside_b, yside_b))
    halo = Halo(field_a, side_landings(xside_a, yside_a), (hsend, hrecv), 0)
    halo.start()
    for field in fields:
        clear_halo(field)
    for side in sides:
        clear_sides(*side)
    dz[...] = z_matrix()

    for t in range(1, STEPS):
        now, nxt = fields[(t - 1) % 2], fields[t % 2]
        xside, yside = sides[(t - 1) % 2]
        last = t == STEPS - 1
        z_terms(now, dz, zterm)

        def update(x, _):
            for half in range(2):
                lanes = pl.ds(half * 128, 128)
                for tile in range(4):
                    rows, inner = pl.ds(tile * 8, 8), pl.ds(8 + tile * 8, 8)
                    centre = now[x + 4, half, inner, :]
                    before = pressure[x, rows, lanes] if t == 1 else nxt[x + 4, half, inner, :]
                    new = 2.0 * centre - before
                    new = new + courant[x, rows, lanes] * laplacian(now, zterm, x, half, tile)
                    new = new + later[t - 1, x, half, rows, :]
                    seen = snapshots[0, x, rows, lanes] * centre if t == 1 else image[x, rows, lanes]
                    image[x, rows, lanes] = seen + snapshots[t, x, rows, lanes] * new
                    if last:
                        out[x, rows, lanes] = new
                    else:
                        nxt[x + 4, half, inner, :] = new
            return 0

        lax.fori_loop(0, 32, update, 0)
        halo.wait()
        if last:
            break

        def add(x, half, tile, terms):
            lanes, rows, inner = pl.ds(half * 128, 128), pl.ds(tile * 8, 8), pl.ds(8 + tile * 8, 8)
            more = courant[x, rows, lanes] * terms
            nxt[x + 4, half, inner, :] = nxt[x + 4, half, inner, :] + more
            image[x, rows, lanes] = image[x, rows, lanes] + snapshots[t, x, rows, lanes] * more

        def y_faces(x, _):
            for half in range(2):
                for tile in (0, 3):
                    add(x, half, tile, y_face_terms(yside, x, half, tile))
            return 0

        def x_faces(tile, _):
            for half in range(2):
                for side in range(2):
                    for layer in range(4):
                        x = layer if side == 0 else 31 - layer
                        add(x, half, tile, x_face_terms(xside, side, layer, half, tile))
            return 0

        lax.fori_loop(0, 32, y_faces, 0)
        lax.fori_loop(0, 4, x_faces, 0)
        halo = Halo(nxt, side_landings(*sides[t % 2]), (hsend, hrecv), t)
        halo.start()


def last_kernel(
    now, out, image_in, xside, yside, courant, snapshots, pressure_hbm, previous_hbm, image_hbm,
    pressure, image, out_sem,
):
    stores = [
        pltpu.make_async_copy(
            now.at[pl.ds(4, 32), half, pl.ds(8, 32), :],
            previous_hbm.at[:, :, pl.ds(half * 128, 128)], out_sem.at[half],
        )
        for half in range(2)
    ]
    for copy in stores:
        copy.start()

    def one(x, side, layer):
        for half in range(2):
            for tile in range(4):
                lanes, rows = pl.ds(half * 128, 128), pl.ds(tile * 8, 8)
                new, seen = out[x, rows, lanes], image_in[x, rows, lanes]
                terms = y_face_terms(yside, x, half, tile) if tile in (0, 3) else None
                if layer is not None:
                    more = x_face_terms(xside, side, layer, half, tile)
                    terms = more if terms is None else terms + more
                if terms is not None:
                    more = courant[x, rows, lanes] * terms
                    new = new + more
                    seen = seen + snapshots[STEPS - 1, x, rows, lanes] * more
                pressure[x, rows, lanes] = new
                image[x, rows, lanes] = seen

    def body(x, _):
        one(x, None, None)
        return 0

    for part in range(4):
        if part == 0:
            for layer in range(4):
                one(layer, 0, layer)
        lax.fori_loop(max(4, part * 8), min(28, part * 8 + 8), body, 0)
        if part == 3:
            for layer in range(4):
                one(31 - layer, 1, layer)
        xs = pl.ds(part * 8, 8)
        stores += [
            pltpu.make_async_copy(pressure.at[xs], pressure_hbm.at[xs], out_sem.at[2 + 2 * part]),
            pltpu.make_async_copy(image.at[xs], image_hbm.at[xs], out_sem.at[3 + 2 * part]),
        ]
        stores[-2].start()
        stores[-1].start()
    for copy in stores:
        copy.wait()


def local(pressure, previous, courant, snapshots, traces, cell_offsets, live_counts):
    f32 = jnp.float32
    vmem, anywhere = pl.BlockSpec(memory_space=pltpu.VMEM), pl.BlockSpec(memory_space=pl.ANY)
    hbm = pl.BlockSpec(memory_space=pltpu.HBM)
    dma, xside, yside = pltpu.SemaphoreType.DMA, (2, 4, 2, 32, 128), (2, 32, 2, 16, 128)
    block, wide = jax.ShapeDtypeStruct((32, 32, 256), f32), jax.ShapeDtypeStruct(FIELD, f32)
    values, codes, hom, pressure, courant = pl.pallas_call(
        deliver_kernel,
        out_shape=(
            jax.ShapeDtypeStruct((NX, NY, 4, 128), f32),
            jax.ShapeDtypeStruct((NX, NY, 1, 128), jnp.int32),
            jax.ShapeDtypeStruct(BLOCK, f32),
            block,
            block,
        ),
        in_specs=[hbm] * 6,
        out_specs=(anywhere, anywhere, vmem, vmem, vmem),
        scratch_shapes=[
            pltpu.VMEM((128, 128), jnp.int32),
            pltpu.VMEM((1, 128), jnp.int32),
            pltpu.VMEM((8, 2, NY, 1, 128), jnp.int32),
            pltpu.VMEM((32, 32, 256), f32),
            pltpu.VMEM((NY, 8, 4, 128), f32),
            pltpu.VMEM((NX, NY, 4, 128), f32),
            pltpu.VMEM((NY, 8, 1, 128), jnp.int32),
            pltpu.VMEM((NX, NY, 1, 128), jnp.int32),
            pltpu.VMEM(FIELD, f32),
            pltpu.VMEM(BLOCK, f32),
            pltpu.VMEM((256, 256), f32),
            dma((5,)),
            dma((4, 2)),
            dma((NY - 1, 2)),
            dma((NY - 1, 2)),
            dma((8, 2)),
            dma((8, 2, 2)),
            dma((8, 2)),
            dma((8, 2, 2)),
            dma((NY - 1, 2)),
            dma((NY - 1, 2)),
            dma((1, 4)),
            dma((1, 4)),
        ],
        compiler_params=pltpu.CompilerParams(
            collective_id=0, has_side_effects=True, vmem_limit_bytes=51300 * 1024
        ),
        name="deliver",
    )(
        traces.reshape(8, 2, NY, 4, 128), cell_offsets.reshape(128, 128), live_counts,
        pressure, previous, courant,
    )
    first, later = pl.pallas_call(
        scatter_kernel,
        out_shape=(jax.ShapeDtypeStruct(BLOCK, f32), jax.ShapeDtypeStruct((3,) + BLOCK, f32)),
        in_specs=[pl.BlockSpec(memory_space=pltpu.SMEM), vmem, vmem],
        out_specs=(vmem, vmem),
        scratch_shapes=[pltpu.VMEM((ROWS, 128), f32)] * K,
        compiler_params=pltpu.CompilerParams(vmem_limit_bytes=38000 * 1024),
        name="scatter",
    )(codes.reshape(128, 128), values.reshape(128, 4, 128), hom)
    now, out, image, xfaces, yfaces = pl.pallas_call(
        steps_kernel,
        out_shape=(wide, block, block, jax.ShapeDtypeStruct(xside, f32), jax.ShapeDtypeStruct(yside, f32)),
        in_specs=[vmem] * 5,
        out_specs=(vmem,) * 5,
        scratch_shapes=[
            pltpu.VMEM(FIELD, f32),
            pltpu.VMEM(BLOCK, f32),
            pltpu.VMEM((256, 256), f32),
            pltpu.VMEM(xside, f32),
            pltpu.VMEM(yside, f32),
            dma((3, 4)),
            dma((3, 4)),
        ],
        compiler_params=pltpu.CompilerParams(
            collective_id=1, has_side_effects=True, vmem_limit_bytes=24000 * 1024
        ),
        name="steps",
    )(first, pressure, courant, snapshots, later)
    return pl.pallas_call(
        last_kernel,
        out_shape=(block, block, block),
        in_specs=[vmem] * 7,
        out_specs=(hbm,) * 3,
        scratch_shapes=[pltpu.VMEM((32, 32, 256), f32)] * 2 + [dma((10,))],
        compiler_params=pltpu.CompilerParams(vmem_limit_bytes=24000 * 1024),
        name="last",
    )(now, out, image, xfaces, yfaces, courant, snapshots)


def solution(mesh):
    field = P("gx", "gy", None)
    return jax.shard_map(
        local,
        mesh=mesh,
        in_specs=(
            field,
            field,
            field,
            P(None, "gx", "gy", None),
            P(("gx", "gy"), None, None, None),
            P(("gx", "gy"), None, None),
            P(("gx", "gy"), None),
        ),
        out_specs=(field, field, field),
        check_vma=False,
    )
```

time: 79.7 us -> 79.2 us (level)
  Pallas kernels: 76.1 us -> 74.9 us
    pallas_call x1, Pallas kernels: 2.64 us -> 1.74 us  [local(): pl.pallas_call(last_kernel, out_shape=(block, block, block), in_specs=[vm...]
where the time goes in v3:
time: 79.2 us; the launch traced here: 78.4 us
  Pallas kernels  74.9 us (95%)
  local copies, waits for them, and re-layouts  2.82 us (4%)
    pallas_call x1, Pallas kernels, local(): pl.pallas_call(scatter_kernel, out_shape=(jax.ShapeDtypeStruct(BLOCK, f32...  27.6 us
    pallas_call x1, Pallas kernels, local(): pl.pallas_call(steps_kernel, out_shape=(wide, block, block, jax.ShapeDtyp...  22.9 us
    pallas_call x1, Pallas kernels, local(): pl.pallas_call(deliver_kernel, out_shape=(jax.ShapeDtypeStruct((NX, NY, 4...  22.6 us
    unnamed x8, local copies, waits for them, and re-layouts  2.82 us
    pallas_call x1, Pallas kernels, local(): pl.pallas_call(last_kernel, out_shape=(block, block, block), in_specs=[vm...  1.74 us

profile of v3, /device:TPU:6, one launch (start us, length us, event | category | flops | bytes accessed | tf_op | source)
XLA Modules:
  0.0 78.4 jit_solution(16964745153888219177)
XLA Ops:
  0.6 0.0 copy-start
  0.6 0.0 copy-start.1
  0.7 1.1 %copy-done.1 = f32[1,128,4,128]{3,2,1,0:T(4,128)S(1)} copy-done((f32[1,128,4,128]{3,2,1,0:T(4,128)S(1)}, f32[1,128,4,128]{3,2,1,0:T(4,128)}, u32[]{:S(2)}) %copy-start.1) | copy-done | bytes 262168
  1.7 0.0 copy-start.2
  1.7 1.1 %copy-done.2 = s32[1,128,128]{2,1,0:T(8,128)S(1)} copy-done((s32[1,128,128]{2,1,0:T(8,128)S(1)}, s32[1,128,128]{2,1,0:T(8,128)}, u32[]{:S(2)}) %copy-start.2) | copy-done | bytes 65560
  2.8 0.0 copy-start.3
  2.8 0.7 copy-done.3
  3.5 22.6 %deliver.1 = (f32[16,8,4,128]{3,2,1,0:T(4,128)S(1)}, s32[16,8,1,128]{3,2,1,0:T(1,128)S(1)}, f32[32,2,32,128]{3,2,1,0:T(8,128)S(1)}, f32[32,32,256]{2,1,0:T(8,128)S(1)}, f32[32,32,256]{2,1,0:T(8,128)S(1)}) custom-call(f32[8,2,8,4,128]{4,3,2,1,0:T(4,128)S(1)} %bitcast.4, s32[128,128]{1,0:T(8,128)S(1)} %bitcast.6, s32[1,128]{1,0:T(1,128)S(1)} %copy-done.3, ...), custom_call_target="tpu_custom_call" | custom-call | tf_op jit(solution)/shard_map/deliver/pallas_call | solution.py:526
  26.0 27.6 %scatter.1 = (f32[32,2,32,128]{3,2,1,0:T(8,128)S(1)}, f32[3,32,2,32,128]{4,3,2,1,0:T(8,128)S(1)}) custom-call(s32[128,128]{1,0:T(8,128)S(1)} %bitcast.7, f32[128,4,128]{2,1,0:T(4,128)S(1)} %bitcast.5, f32[32,2,32,128]{3,2,1,0:T(8,128)S(1)} %get-tuple-element.17.hom), custom_call_target="tpu_custom_call" | custom-call | tf_op jit(solution)/shard_map/scatter/pallas_call | solution.py:570
  53.7 0.0 copy-done
  53.7 22.9 %steps.1 = (f32[40,2,48,128]{3,2,1,0:T(8,128)S(1)}, f32[32,32,256]{2,1,0:T(8,128)S(1)}, f32[32,32,256]{2,1,0:T(8,128)S(1)}, f32[2,4,2,32,128]{4,3,2,1,0:T(8,128)S(1)}, f32[2,32,2,16,128]{4,3,2,1,0:T(8,128)S(1)}) custom-call(f32[32,2,32,128]{3,2,1,0:T(8,128)S(1)} %get-tuple-element.18.first, f32[32,32,256]{2,1,0:T(8,128)S(1)} %get-tuple-element.19.pressure, ...), custom_call_target="tpu_custom_call" | custom-call | tf_op jit(solution)/shard_map/steps/pallas_call | solution.py:579
  76.6 1.7 %last.1 = (f32[32,32,256]{2,1,0:T(8,128)}, f32[32,32,256]{2,1,0:T(8,128)}, f32[32,32,256]{2,1,0:T(8,128)}) custom-call(f32[40,2,48,128]{3,2,1,0:T(8,128)S(1)} %get-tuple-element.22.now, f32[32,32,256]{2,1,0:T(8,128)S(1)} %get-tuple-element.23.out, f32[32,32,256]{2,1,0:T(8,128)S(1)} %get-tuple-element.24.image_in, ...), custom_call_target="tpu_custom_call" | custom-call | tf_op jit(solution)/shard_map/last/pallas_call | solution.py:598
Async XLA Ops:
  0.6 53.0 %copy-start = (f32[4,32,32,256]{3,2,1,0:T(8,128)S(1)}, f32[4,32,32,256]{3,2,1,0:T(8,128)}, u32[]{:S(2)}) copy-start(f32[4,32,32,256]{3,2,1,0:T(8,128)} %snapshots.3) | copy-start | bytes 12582916
  0.6 1.1 %copy-start.1 = (f32[1,128,4,128]{3,2,1,0:T(4,128)S(1)}, f32[1,128,4,128]{3,2,1,0:T(4,128)}, u32[]{:S(2)}) copy-start(f32[1,128,4,128]{3,2,1,0:T(4,128)} %param.11) | copy-start | bytes 786436
  1.7 1.1 %copy-start.2 = (s32[1,128,128]{2,1,0:T(8,128)S(1)}, s32[1,128,128]{2,1,0:T(8,128)}, u32[]{:S(2)}) copy-start(s32[1,128,128]{2,1,0:T(8,128)} %param.12) | copy-start | bytes 196612
  2.8 0.7 copy-start.3

commit v4 on v3

--- a/solution.py
+++ b/solution.py
@@ -10,7 +10,7 @@
 STEPS = 4
 COEFS = (-205.0 / 72.0, 8.0 / 5.0, -1.0 / 5.0, 8.0 / 315.0, -1.0 / 560.0)
 NX, NY = 16, 8
-K = 5
+K = 6
 ROWS = 8192 + 16
 MESH = pl.DeviceIdType.MESH
 FIELD = (40, 2, 48, 128)
@@ -185,7 +185,7 @@
     counts = jnp.broadcast_to(live[...].astype(jnp.float32), (128, 128)).T.astype(jnp.int32)
     cells = offsets[...]
     margin = 8 - 4 * lax.rem(b, 2)
-    code = (((cells >> 7) * 4 + margin) << 8) | (cells & 127) | jnp.where(lane < counts, 0, 128)
+    code = (((cells >> 7) * 4 + margin) << 8) | jnp.where(lane < counts, cells & 127, 255)
     codes[...] = code.reshape(8, 2, NY, 1, 128)
     clear_field_edges(field)
     pl.semaphore_wait(sem, len(peers))
@@ -335,7 +335,7 @@
             copy.wait()
 
 
-def scatter_kernel(codes, values, hom, first, later, *sums):
+def clear_sums(sums):
     zero = jnp.zeros((64, 128), jnp.float32)
 
     def clear(i, _):
@@ -346,44 +346,68 @@
     lax.fori_loop(0, 128, clear, 0)
     for total in sums:
         total[pl.ds(8192, 16), :] = jnp.zeros((16, 128), jnp.float32)
+
+
+def scatter_kernel(codes, values, *rest):
+    sums = rest[:K]
+    rows_all, lanes_all, rows0, rows1, lanes0, lanes1, sems = rest[K:]
+    rows_all[...] = codes[...] >> 8
+    word = codes[pl.ds(0, 32, stride=4), :] & 255
+    for q in range(1, 4):
+        word = word | ((codes[pl.ds(q, 32, stride=4), :] & 255) << (8 * q))
+    lanes_all[...] = word
+    blocks = ((rows0, lanes0), (rows1, lanes1))
+
+    def fetch(group, n):
+        rows, lanes = blocks[n]
+        return (
+            pltpu.make_async_copy(rows_all.at[pl.ds(4 * group, 4)], rows, sems.at[n, 0]),
+            pltpu.make_async_copy(lanes_all.at[pl.ds(group, 1)], lanes, sems.at[n, 1]),
+        )
+
+    for n in range(2):
+        for copy in fetch(n, n):
+            copy.start()
+    clear_sums(sums)
     sub = lax.broadcasted_iota(jnp.int32, (8, 128), 0)
     lane = lax.broadcasted_iota(jnp.int32, (8, 128), 1)
-    place = (jnp.where(sub < 4, lane, -1), jnp.where(sub < 4, -1, lane))
-
-    def body(s, _):
-        both = jnp.concatenate([values[2 * s], values[2 * s + 1]], axis=0)
-        for j in range(128):
-            wide = jnp.broadcast_to(both[:, j : j + 1], (8, 128))
-            for h in range(2):
-                code = codes[2 * s + h, j]
-                rows = pl.ds(code >> 8, 8)
-                cell = jnp.full((8, 128), code, jnp.int32) & 255
-                total = sums[(2 * j + h) % K]
-                total[rows, :] = total[rows, :] + jnp.where(place[h] == cell, wide, 0.0)
+    place = (jnp.where(sub < 4, lane, 128), jnp.where(sub < 4, 128, lane))
+    place = [place[q % 2] << (8 * q) for q in range(4)]
+    bits = (255, 255 << 8, 255 << 16, -(1 << 24))
+
+    def body(i, _):
+        for n in range(2):
+            group = 2 * i + n
+            for copy in fetch(group, n):
+                copy.wait()
+            rows, lanes = blocks[n]
+            pairs = [
+                jnp.concatenate([values[4 * group + 2 * p], values[4 * group + 2 * p + 1]], axis=0) for p in range(2)
+            ]
+            for j in range(128):
+                wide = [jnp.broadcast_to(pair[:, j : j + 1], (8, 128)) for pair in pairs]
+                cells = jnp.full((8, 128), lanes[0, j], jnp.int32)
+                for q in range(4):
+                    window = pl.ds(rows[q, j], 8)
+                    total = sums[(4 * j + q) % K]
+                    more = jnp.where((cells & bits[q]) == place[q], wide[q // 2], 0.0)
+                    total[window, :] = total[window, :] + more
+
+            @pl.when(i < 15)
+            def _():
+                for copy in fetch(group + 2, n):
+                    copy.start()
         return 0
 
-    lax.fori_loop(0, 64, body, 0)
-
-    def finish(i, _):
-        rows = pl.ds(pl.multiple_of(i * 64 + 8, 8), 64)
-        total = sums[0][rows, :]
-        for other in sums[1:]:
-            total = total + other[rows, :]
-        turned = jnp.swapaxes(total.reshape(8, 8, 128), 0, 1)
-        x, ys = i // 4, pl.ds(pl.multiple_of(i % 4 * 8, 8), 8)
-        for half in range(2):
-            first[x, half, ys, :] = hom[x, half, ys, :] + turned[half * 4]
-            for t in range(1, STEPS):
-                later[t - 1, x, half, ys, :] = turned[half * 4 + t]
-        return 0
-
-    lax.fori_loop(0, 128, finish, 0)
+    lax.fori_loop(0, 16, body, 0)
 
 
 def steps_kernel(
-    first, pressure, courant, snapshots, later, field_a, out, image, xside_a, yside_a,
-    field_b, zterm, dz, xside_b, yside_b, hsend, hrecv,
+    *refs,
 ):
+    sums, refs = refs[:K], refs[K:]
+    (hom, pressure, courant, field_a, field_b, first, out, xside_a, yside_a, later,
+     zterm, dz, xside_b, yside_b, hsend, hrecv) = refs
     a, b = lax.axis_index("gx"), lax.axis_index("gy")
     sem = pltpu.get_barrier_semaphore()
     near = (("gy", b - 1, b > 0), ("gy", b + 1, b < NY - 1), ("gx", a - 1, a > 0), ("gx", a + 1, a < NX - 1))
@@ -392,12 +416,23 @@
         def _():
             pl.semaphore_signal(sem, inc=1, device_id={axis: device}, device_id_type=MESH)
 
-    def load(x, _):
+    def finish(i, _):
+        rows = pl.ds(pl.multiple_of(i * 64 + 8, 8), 64)
+        total = sums[0][rows, :]
+        for other in sums[1:]:
+            total = total + other[rows, :]
+        turned = jnp.swapaxes(total.reshape(8, 8, 128), 0, 1)
+        x, y = i // 4, i % 4 * 8
         for half in range(2):
-            field_a[x + 4, half, pl.ds(8, 32), :] = first[x, half]
+            ys = pl.ds(pl.multiple_of(y, 8), 8)
+            new = hom[x, half, ys, :] + turned[half * 4]
+            first[x, half, ys, :] = new
+            field_a[x + 4, half, pl.ds(pl.multiple_of(y + 8, 8), 8), :] = new
+            for t in range(1, STEPS):
+                later[t - 1, x, half, ys, :] = turned[half * 4 + t]
         return 0
 
-    lax.fori_loop(0, 32, load, 0)
+    lax.fori_loop(0, 128, finish, 0)
     pl.semaphore_wait(sem, sum(there.astype(jnp.int32) for _, _, there in near))
 
     fields, sides = (field_a, field_b), ((xside_a, yside_a), (xside_b, yside_b))
@@ -425,8 +460,6 @@
                     new = 2.0 * centre - before
                     new = new + courant[x, rows, lanes] * laplacian(now, zterm, x, half, tile)
                     new = new + later[t - 1, x, half, rows, :]
-                    seen = snapshots[0, x, rows, lanes] * centre if t == 1 else image[x, rows, lanes]
-                    image[x, rows, lanes] = seen + snapshots[t, x, rows, lanes] * new
                     if last:
                         out[x, rows, lanes] = new
                     else:
@@ -442,7 +475,6 @@
             lanes, rows, inner = pl.ds(half * 128, 128), pl.ds(tile * 8, 8), pl.ds(8 + tile * 8, 8)
             more = courant[x, rows, lanes] * terms
             nxt[x + 4, half, inner, :] = nxt[x + 4, half, inner, :] + more
-            image[x, rows, lanes] = image[x, rows, lanes] + snapshots[t, x, rows, lanes] * more
 
         def y_faces(x, _):
             for half in range(2):
@@ -465,7 +497,7 @@
 
 
 def last_kernel(
-    now, out, image_in, xside, yside, courant, snapshots, pressure_hbm, previous_hbm, image_hbm,
+    now, before, first, out, xside, yside, courant, snapshots, pressure_hbm, previous_hbm, image_hbm,
     pressure, image, out_sem,
 ):
     stores = [
@@ -482,17 +514,19 @@
         for half in range(2):
             for tile in range(4):
                 lanes, rows = pl.ds(half * 128, 128), pl.ds(tile * 8, 8)
-                new, seen = out[x, rows, lanes], image_in[x, rows, lanes]
+                inner = pl.ds(8 + tile * 8, 8)
+                new = out[x, rows, lanes]
                 terms = y_face_terms(yside, x, half, tile) if tile in (0, 3) else None
                 if layer is not None:
                     more = x_face_terms(xside, side, layer, half, tile)
                     terms = more if terms is None else terms + more
                 if terms is not None:
-                    more = courant[x, rows, lanes] * terms
-                    new = new + more
-                    seen = seen + snapshots[STEPS - 1, x, rows, lanes] * more
+                    new = new + courant[x, rows, lanes] * terms
                 pressure[x, rows, lanes] = new
-                image[x, rows, lanes] = seen
+                seen = snapshots[0, x, rows, lanes] * first[x, half, rows, :]
+                seen = seen + snapshots[1, x, rows, lanes] * before[x + 4, half, inner, :]
+                seen = seen + snapshots[2, x, rows, lanes] * now[x + 4, half, inner, :]
+                image[x, rows, lanes] = seen + snapshots[3, x, rows, lanes] * new
 
     def body(x, _):
         one(x, None, None)
@@ -567,22 +601,37 @@
         traces.reshape(8, 2, NY, 4, 128), cell_offsets.reshape(128, 128), live_counts,
         pressure, previous, courant,
     )
-    first, later = pl.pallas_call(
+    sums = pl.pallas_call(
         scatter_kernel,
-        out_shape=(jax.ShapeDtypeStruct(BLOCK, f32), jax.ShapeDtypeStruct((3,) + BLOCK, f32)),
-        in_specs=[pl.BlockSpec(memory_space=pltpu.SMEM), vmem, vmem],
-        out_specs=(vmem, vmem),
-        scratch_shapes=[pltpu.VMEM((ROWS, 128), f32)] * K,
-        compiler_params=pltpu.CompilerParams(vmem_limit_bytes=38000 * 1024),
+        out_shape=(jax.ShapeDtypeStruct((ROWS, 128), f32),) * K,
+        in_specs=[vmem, vmem],
+        out_specs=(vmem,) * K,
+        scratch_shapes=[
+            pltpu.VMEM((128, 128), jnp.int32),
+            pltpu.VMEM((32, 128), jnp.int32),
+            pltpu.SMEM((4, 128), jnp.int32),
+            pltpu.SMEM((4, 128), jnp.int32),
+            pltpu.SMEM((1, 128), jnp.int32),
+            pltpu.SMEM((1, 128), jnp.int32),
+            dma((2, 2)),
+        ],
+        compiler_params=pltpu.CompilerParams(vmem_limit_bytes=8000 * 1024),
         name="scatter",
-    )(codes.reshape(128, 128), values.reshape(128, 4, 128), hom)
-    now, out, image, xfaces, yfaces = pl.pallas_call(
+    )(codes.reshape(128, 128), values.reshape(128, 4, 128))
+    now, before, first, out, xfaces, yfaces = pl.pallas_call(
         steps_kernel,
-        out_shape=(wide, block, block, jax.ShapeDtypeStruct(xside, f32), jax.ShapeDtypeStruct(yside, f32)),
-        in_specs=[vmem] * 5,
-        out_specs=(vmem,) * 5,
+        out_shape=(
+            wide,
+            wide,
+            jax.ShapeDtypeStruct(BLOCK, f32),
+            block,
+            jax.ShapeDtypeStruct(xside, f32),
+            jax.ShapeDtypeStruct(yside, f32),
+        ),
+        in_specs=[vmem] * (K + 3),
+        out_specs=(vmem,) * 6,
         scratch_shapes=[
-            pltpu.VMEM(FIELD, f32),
+            pltpu.VMEM((3,) + BLOCK, f32),
             pltpu.VMEM(BLOCK, f32),
             pltpu.VMEM((256, 256), f32),
             pltpu.VMEM(xside, f32),
@@ -591,19 +640,19 @@
             dma((3, 4)),
         ],
         compiler_params=pltpu.CompilerParams(
-            collective_id=1, has_side_effects=True, vmem_limit_bytes=24000 * 1024
+            collective_id=1, has_side_effects=True, vmem_limit_bytes=10000 * 1024
         ),
         name="steps",
-    )(first, pressure, courant, snapshots, later)
+    )(*sums, hom, pressure, courant)
     return pl.pallas_call(
         last_kernel,
         out_shape=(block, block, block),
-        in_specs=[vmem] * 7,
+        in_specs=[vmem] * 8,
         out_specs=(hbm,) * 3,
         scratch_shapes=[pltpu.VMEM((32, 32, 256), f32)] * 2 + [dma((10,))],
-        compiler_params=pltpu.CompilerParams(vmem_limit_bytes=24000 * 1024),
+        compiler_params=pltpu.CompilerParams(vmem_limit_bytes=6000 * 1024),
         name="last",
-    )(now, out, image, xfaces, yfaces, courant, snapshots)
+    )(now, before, first, out, xfaces, yfaces, courant, snapshots)
 
 
 def solution(mesh):

time: 79.2 us -> 70.4 us (0.89)
  Pallas kernels: 74.9 us -> 66.6 us
    pallas_call x2, Pallas kernels: 50.6 us -> 42.3 us  [the longest x1 21.7 us: local(): pl.pallas_call(steps_kernel, out_shape=(wide, wide, jax.ShapeDtypeStruct(...]
where the time goes in v4:
time: 70.4 us; the launch traced here: 69.7 us
  Pallas kernels  66.6 us (95%)
  local copies, waits for them, and re-layouts  2.44 us (3%)
    pallas_call x1, Pallas kernels, local(): pl.pallas_call(deliver_kernel, out_shape=(jax.ShapeDtypeStruct((NX, NY, 4...  22.6 us
    pallas_call x1, Pallas kernels, local(): pl.pallas_call(steps_kernel, out_shape=(wide, wide, jax.ShapeDtypeStruct(...  21.7 us
    pallas_call x1, Pallas kernels, local(): pl.pallas_call(scatter_kernel, out_shape=(jax.ShapeDtypeStruct((ROWS, 128...  20.6 us
    unnamed x8, local copies, waits for them, and re-layouts  2.44 us
    pallas_call x1, Pallas kernels, local(): pl.pallas_call(last_kernel, out_shape=(block, block, block), in_specs=[vm...  1.74 us

profile of v4, /device:TPU:6, one launch (start us, length us, event | category | flops | bytes accessed | tf_op | source)
XLA Modules:
  0.0 69.7 jit_solution(17840434661950651598)
XLA Ops:
  0.6 0.0 copy-start.1
  0.6 0.9 %copy-done.1 = f32[1,128,4,128]{3,2,1,0:T(4,128)S(1)} copy-done((f32[1,128,4,128]{3,2,1,0:T(4,128)S(1)}, f32[1,128,4,128]{3,2,1,0:T(4,128)}, u32[]{:S(2)}) %copy-start.1) | copy-done | bytes 262168
  1.6 0.0 copy-start.2
  1.6 0.8 %copy-done.2 = s32[1,128,128]{2,1,0:T(8,128)S(1)} copy-done((s32[1,128,128]{2,1,0:T(8,128)S(1)}, s32[1,128,128]{2,1,0:T(8,128)}, u32[]{:S(2)}) %copy-start.2) | copy-done | bytes 65560
  2.4 0.0 copy-start.3
  2.4 0.7 copy-done.3
  3.1 22.6 %deliver.1 = (f32[16,8,4,128]{3,2,1,0:T(4,128)S(1)}, s32[16,8,1,128]{3,2,1,0:T(1,128)S(1)}, f32[32,2,32,128]{3,2,1,0:T(8,128)S(1)}, f32[32,32,256]{2,1,0:T(8,128)S(1)}, f32[32,32,256]{2,1,0:T(8,128)S(1)}) custom-call(f32[8,2,8,4,128]{4,3,2,1,0:T(4,128)S(1)} %bitcast.4, s32[128,128]{1,0:T(8,128)S(1)} %bitcast.6, s32[1,128]{1,0:T(1,128)S(1)} %copy-done.3, ...), custom_call_target="tpu_custom_call" | custom-call | tf_op jit(solution)/shard_map/deliver/pallas_call | solution.py:560
  25.6 20.6 %scatter.1 = (f32[8208,128]{1,0:T(8,128)S(1)}, f32[8208,128]{1,0:T(8,128)S(1)}, f32[8208,128]{1,0:T(8,128)S(1)}, f32[8208,128]{1,0:T(8,128)S(1)}, f32[8208,128]{1,0:T(8,128)S(1)}, /*index=5*/f32[8208,128]{1,0:T(8,128)S(1)}) custom-call(s32[128,128]{1,0:T(8,128)S(1)} %bitcast.7, f32[128,4,128]{2,1,0:T(4,128)S(1)} %bitcast.5), custom_call_target="tpu_custom_call" | custom-call | tf_op jit(solution)/shard_map/scatter/pallas_call | solution.py:604
  46.3 0.0 copy-start
  46.3 21.7 %steps.1 = (f32[40,2,48,128]{3,2,1,0:T(8,128)S(1)}, f32[40,2,48,128]{3,2,1,0:T(8,128)S(1)}, f32[32,2,32,128]{3,2,1,0:T(8,128)S(1)}, f32[32,32,256]{2,1,0:T(8,128...) custom-call(f32[8208,128]{1,0:T(8,128)S(1)} %get-tuple-element.22.refs_0_, ...), custom_call_target="tpu_custom_call" | custom-call | tf_op jit(solution)/shard_map/steps/pallas_call | solution.py:621
  68.0 0.0 copy-done
  68.0 1.7 %last.1 = (f32[32,32,256]{2,1,0:T(8,128)}, f32[32,32,256]{2,1,0:T(8,128)}, f32[32,32,256]{2,1,0:T(8,128)}) custom-call(f32[40,2,48,128]{3,2,1,0:T(8,128)S(1)} %get-tuple-element.31.now, f32[40,2,48,128]{3,2,1,0:T(8,128)S(1)} %get-tuple-element.32.before, f32[32,2,32,128]{3,2,1,0:T(8,128)S(1)} %get-tuple-element.33.first, ...), custom_call_target="tpu_custom_call" | custom-call | tf_op jit(solution)/shard_map/last/pallas_call | solution.py:647
Async XLA Ops:
  0.6 1.0 %copy-start.1 = (f32[1,128,4,128]{3,2,1,0:T(4,128)S(1)}, f32[1,128,4,128]{3,2,1,0:T(4,128)}, u32[]{:S(2)}) copy-start(f32[1,128,4,128]{3,2,1,0:T(4,128)} %param.11) | copy-start | bytes 786436
  1.6 0.8 %copy-start.2 = (s32[1,128,128]{2,1,0:T(8,128)S(1)}, s32[1,128,128]{2,1,0:T(8,128)}, u32[]{:S(2)}) copy-start(s32[1,128,128]{2,1,0:T(8,128)} %param.12) | copy-start | bytes 196612
  2.4 0.7 copy-start.3
  46.3 21.7 %copy-start = (f32[4,32,32,256]{3,2,1,0:T(8,128)S(1)}, f32[4,32,32,256]{3,2,1,0:T(8,128)}, u32[]{:S(2)}) copy-start(f32[4,32,32,256]{3,2,1,0:T(8,128)} %snapshots.1) | copy-start | bytes 12582916

commit v5 on v4

--- a/solution.py
+++ b/solution.py
@@ -159,8 +159,8 @@
 
 def deliver_kernel(
     traces, offsets_hbm, live_hbm, pressure_hbm, previous_hbm, courant_hbm,
-    values_out, codes_out, hom, pressure, courant,
-    offsets, live, codes, previous, mid_values0, mid_values1, mid_codes0, mid_codes1, field, zterm, dz,
+    values_out, hom, pressure, courant,
+    offsets, live, slots, previous, mid_values0, mid_values1, field, zterm, dz,
     load_sem, local_sem, send1, recv1, send2, recv2, send3, recv3, send4, recv4, hsend, hrecv,
 ):
     a, b = lax.axis_index("gx"), lax.axis_index("gy")
@@ -168,7 +168,7 @@
         pltpu.make_async_copy(src, dst, load_sem.at[i])
         for i, (src, dst) in enumerate((
             (offsets_hbm, offsets), (live_hbm, live), (pressure_hbm, pressure),
-            (previous_hbm, previous), (courant_hbm, courant),
+            (previous_hbm, previous), (courant_hbm, courant), (traces, slots.at[:, :, :, pl.ds(0, 4)]),
         ))
     ]
     for copy in loads:
@@ -186,12 +186,13 @@
     cells = offsets[...]
     margin = 8 - 4 * lax.rem(b, 2)
     code = (((cells >> 7) * 4 + margin) << 8) | jnp.where(lane < counts, cells & 127, 255)
-    codes[...] = code.reshape(8, 2, NY, 1, 128)
+    slots[:, :, :, 4] = code.astype(jnp.float32).reshape(8, 2, NY, 1, 128)
+    loads[5].wait()
     clear_field_edges(field)
     pl.semaphore_wait(sem, len(peers))
 
     core, pair = lax.rem(a, 2), a // 2
-    both = ((traces, mid_values0, mid_values1, values_out), (codes, mid_codes0, mid_codes1, codes_out))
+    both = ((slots, mid_values0, mid_values1, values_out),)
 
     def remote(src, dst, send, recv, device):
         return pltpu.make_async_remote_copy(
@@ -227,21 +228,18 @@
     def gx_arrived(recv, landing):
         for o in range(8):
             for sender in range(2):
-                for kind in range(2):
-                    def wait():
-                        remote(
-                            landing[kind], landing[kind], send2.at[o, kind], recv.at[o, sender, kind], {"gx": a}
-                        ).wait_recv()
-
-                    if o > 0:
-                        wait()
-                    else:
-                        pl.when(core != sender)(wait)
-
-    for n in range(16):
-        if n < 14:
+                def wait():
+                    remote(landing, landing, send2.at[o, 0], recv.at[o, sender, 0], {"gx": a}).wait_recv()
+
+                if o > 0:
+                    wait()
+                else:
+                    pl.when(core != sender)(wait)
+
+    for n in range(8):
+        if n < 7:
             gy_first[n].start()
-        if n >= 2:
+        if n >= 1:
             gx_first[n].start()
     for copy in own_first:
         copy.start()
@@ -249,12 +247,10 @@
     @pl.when(core == 0)
     def _():
         gx_first[0].start()
-        gx_first[1].start()
 
     @pl.when(core == 1)
     def _():
         own_gx_first[0].start()
-        own_gx_first[1].start()
 
     loads[2].wait()
 
@@ -274,21 +270,18 @@
         copy.wait()
     for copy in gy_first:
         copy.wait_recv()
-    for copy in gx_second[2:]:
+    for copy in gx_second[1:]:
         copy.start()
 
     @pl.when(core == 0)
     def _():
         own_gx_second[0].start()
-        own_gx_second[1].start()
 
     @pl.when(core == 1)
     def _():
         gx_second[0].start()
-        gx_second[1].start()
         own_gx_first[0].wait()
-        own_gx_first[1].wait()
-        gx_arrived(recv2, (mid_values1.at[0], mid_codes1.at[0]))
+        gx_arrived(recv2, mid_values1.at[0])
         for copy in gy_second:
             copy.start()
         for copy in own_second:
@@ -312,23 +305,20 @@
 
     for copy in gy_first:
         copy.wait_send()
-    for copy in gx_first[2:]:
+    for copy in gx_first[1:]:
         copy.wait_send()
-    for copy in gx_second[2:]:
+    for copy in gx_second[1:]:
         copy.wait_send()
 
     @pl.when(core == 0)
     def _():
         gx_first[0].wait_send()
-        gx_first[1].wait_send()
         own_gx_second[0].wait()
-        own_gx_second[1].wait()
-        gx_arrived(recv3, (values_out.at[0], codes_out.at[0]))
+        gx_arrived(recv3, values_out.at[0])
 
     @pl.when(core == 1)
     def _():
         gx_second[0].wait_send()
-        gx_second[1].wait_send()
         for copy in own_second:
             copy.wait()
         for copy in gy_second:
@@ -348,13 +338,13 @@
         total[pl.ds(8192, 16), :] = jnp.zeros((16, 128), jnp.float32)
 
 
-def scatter_kernel(codes, values, *rest):
+def scatter_kernel(values, *rest):
     sums = rest[:K]
     rows_all, lanes_all, rows0, rows1, lanes0, lanes1, sems = rest[K:]
-    rows_all[...] = codes[...] >> 8
-    word = codes[pl.ds(0, 32, stride=4), :] & 255
-    for q in range(1, 4):
-        word = word | ((codes[pl.ds(q, 32, stride=4), :] & 255) << (8 * q))
+    rows_all[...] = values[pl.ds(4, 128, stride=5), :].astype(jnp.int32) >> 8
+    word = jnp.zeros((32, 128), jnp.int32)
+    for q in range(4):
+        word = word | ((values[pl.ds(5 * q + 4, 32, stride=20), :].astype(jnp.int32) & 255) << (8 * q))
     lanes_all[...] = word
     blocks = ((rows0, lanes0), (rows1, lanes1))
 
@@ -382,7 +372,8 @@
                 copy.wait()
             rows, lanes = blocks[n]
             pairs = [
-                jnp.concatenate([values[4 * group + 2 * p], values[4 * group + 2 * p + 1]], axis=0) for p in range(2)
+                jnp.concatenate([values[pl.ds(20 * group + 10 * p + 5 * n, 4), :] for n in range(2)], axis=0)
+                for p in range(2)
             ]
             for j in range(128):
                 wide = [jnp.broadcast_to(pair[:, j : j + 1], (8, 128)) for pair in pairs]
@@ -557,39 +548,36 @@
     hbm = pl.BlockSpec(memory_space=pltpu.HBM)
     dma, xside, yside = pltpu.SemaphoreType.DMA, (2, 4, 2, 32, 128), (2, 32, 2, 16, 128)
     block, wide = jax.ShapeDtypeStruct((32, 32, 256), f32), jax.ShapeDtypeStruct(FIELD, f32)
-    values, codes, hom, pressure, courant = pl.pallas_call(
+    values, hom, pressure, courant = pl.pallas_call(
         deliver_kernel,
         out_shape=(
-            jax.ShapeDtypeStruct((NX, NY, 4, 128), f32),
-            jax.ShapeDtypeStruct((NX, NY, 1, 128), jnp.int32),
+            jax.ShapeDtypeStruct((NX, NY, 5, 1, 128), f32),
             jax.ShapeDtypeStruct(BLOCK, f32),
             block,
             block,
         ),
         in_specs=[hbm] * 6,
-        out_specs=(anywhere, anywhere, vmem, vmem, vmem),
+        out_specs=(anywhere, vmem, vmem, vmem),
         scratch_shapes=[
             pltpu.VMEM((128, 128), jnp.int32),
             pltpu.VMEM((1, 128), jnp.int32),
-            pltpu.VMEM((8, 2, NY, 1, 128), jnp.int32),
+            pltpu.VMEM((8, 2, NY, 5, 1, 128), f32),
             pltpu.VMEM((32, 32, 256), f32),
-            pltpu.VMEM((NY, 8, 4, 128), f32),
-            pltpu.VMEM((NX, NY, 4, 128), f32),
-            pltpu.VMEM((NY, 8, 1, 128), jnp.int32),
-            pltpu.VMEM((NX, NY, 1, 128), jnp.int32),
+            pltpu.VMEM((NY, 8, 5, 1, 128), f32),
+            pltpu.VMEM((NX, NY, 5, 1, 128), f32),
             pltpu.VMEM(FIELD, f32),
             pltpu.VMEM(BLOCK, f32),
             pltpu.VMEM((256, 256), f32),
-            dma((5,)),
-            dma((4, 2)),
-            dma((NY - 1, 2)),
-            dma((NY - 1, 2)),
-            dma((8, 2)),
-            dma((8, 2, 2)),
-            dma((8, 2)),
-            dma((8, 2, 2)),
-            dma((NY - 1, 2)),
-            dma((NY - 1, 2)),
+            dma((6,)),
+            dma((4, 1)),
+            dma((NY - 1, 1)),
+            dma((NY - 1, 1)),
+            dma((8, 1)),
+            dma((8, 2, 1)),
+            dma((8, 1)),
+            dma((8, 2, 1)),
+            dma((NY - 1, 1)),
+            dma((NY - 1, 1)),
             dma((1, 4)),
             dma((1, 4)),
         ],
@@ -598,13 +586,13 @@
         ),
         name="deliver",
     )(
-        traces.reshape(8, 2, NY, 4, 128), cell_offsets.reshape(128, 128), live_counts,
+        traces.reshape(8, 2, NY, 4, 1, 128), cell_offsets.reshape(128, 128), live_counts,
         pressure, previous, courant,
     )
     sums = pl.pallas_call(
         scatter_kernel,
         out_shape=(jax.ShapeDtypeStruct((ROWS, 128), f32),) * K,
-        in_specs=[vmem, vmem],
+        in_specs=[vmem],
         out_specs=(vmem,) * K,
         scratch_shapes=[
             pltpu.VMEM((128, 128), jnp.int32),
@@ -617,7 +605,7 @@
         ],
         compiler_params=pltpu.CompilerParams(vmem_limit_bytes=8000 * 1024),
         name="scatter",
-    )(codes.reshape(128, 128), values.reshape(128, 4, 128))
+    )(values.reshape(640, 128))
     now, before, first, out, xfaces, yfaces = pl.pallas_call(
         steps_kernel,
         out_shape=(

time: 70.4 us -> 69.8 us (level)
    pallas_call x1, Pallas kernels: 22.6 us -> 21.8 us  [local(): pl.pallas_call(deliver_kernel, out_shape=(jax.ShapeDtypeStruct((NX, NY, 5...]
where the time goes in v5:
time: 69.8 us; the launch traced here: 69.1 us
  Pallas kernels  66 us (95%)
  local copies, waits for them, and re-layouts  2.44 us (3%)
    pallas_call x1, Pallas kernels, local(): pl.pallas_call(deliver_kernel, out_shape=(jax.ShapeDtypeStruct((NX, NY, 5...  21.8 us
    pallas_call x1, Pallas kernels, local(): pl.pallas_call(steps_kernel, out_shape=(wide, wide, jax.ShapeDtypeStruct(...  21.7 us
    pallas_call x1, Pallas kernels, local(): pl.pallas_call(scatter_kernel, out_shape=(jax.ShapeDtypeStruct((ROWS, 128...  20.6 us
    unnamed x8, local copies, waits for them, and re-layouts  2.44 us
    pallas_call x1, Pallas kernels, local(): pl.pallas_call(last_kernel, out_shape=(block, block, block), in_specs=[vm...  1.74 us

profile of v5, /device:TPU:6, one launch (start us, length us, event | category | flops | bytes accessed | tf_op | source)
XLA Modules:
  0.0 69.1 jit_solution(11527872708639147154)
XLA Ops:
  0.6 0.0 copy-start.1
  0.6 0.9 %copy-done.1 = f32[1,128,4,128]{3,2,1,0:T(4,128)S(1)} copy-done((f32[1,128,4,128]{3,2,1,0:T(4,128)S(1)}, f32[1,128,4,128]{3,2,1,0:T(4,128)}, u32[]{:S(2)}) %copy-start.1) | copy-done | bytes 262168
  1.6 0.0 copy-start.2
  1.6 0.8 %copy-done.2 = s32[1,128,128]{2,1,0:T(8,128)S(1)} copy-done((s32[1,128,128]{2,1,0:T(8,128)S(1)}, s32[1,128,128]{2,1,0:T(8,128)}, u32[]{:S(2)}) %copy-start.2) | copy-done | bytes 65560
  2.4 0.0 copy-start.3
  2.4 0.7 copy-done.3
  3.1 21.8 %deliver.1 = (f32[16,8,5,1,128]{4,3,2,1,0:T(1,128)S(1)}, f32[32,2,32,128]{3,2,1,0:T(8,128)S(1)}, f32[32,32,256]{2,1,0:T(8,128)S(1)}, f32[32,32,256]{2,1,0:T(8,128)S(1)}) custom-call(f32[8,2,8,4,1,128]{5,4,3,2,1,0:T(1,128)S(1)} %bitcast.4, s32[128,128]{1,0:T(8,128)S(1)} %bitcast.5, s32[1,128]{1,0:T(1,128)S(1)} %copy-done.3, f32[32,32,256]{2,1,0:T(8,128)} %pressure_hbm.1, ...), custom_call_target="tpu_custom_call" | custom-call | tf_op jit(solution)/shard_map/deliver/pallas_call | solution.py:551
  24.9 20.6 %scatter.1 = (f32[8208,128]{1,0:T(8,128)S(1)}, f32[8208,128]{1,0:T(8,128)S(1)}, f32[8208,128]{1,0:T(8,128)S(1)}, f32[8208,128]{1,0:T(8,128)S(1)}, f32[8208,128]{1,0:T(8,128)S(1)}, /*index=5*/f32[8208,128]{1,0:T(8,128)S(1)}) custom-call(f32[640,128]{1,0:T(8,128)S(1)} %bitcast.3), custom_call_target="tpu_custom_call" | custom-call | tf_op jit(solution)/shard_map/scatter/pallas_call | solution.py:592
  45.6 0.0 copy-start
  45.6 21.7 %steps.1 = (f32[40,2,48,128]{3,2,1,0:T(8,128)S(1)}, f32[40,2,48,128]{3,2,1,0:T(8,128)S(1)}, f32[32,2,32,128]{3,2,1,0:T(8,128)S(1)}, f32[32,32,256]{2,1,0:T(8,128...) custom-call(f32[8208,128]{1,0:T(8,128)S(1)} %get-tuple-element.20.refs_0_, ...), custom_call_target="tpu_custom_call" | custom-call | tf_op jit(solution)/shard_map/steps/pallas_call | solution.py:609
  67.3 0.0 copy-done
  67.3 1.7 %last.1 = (f32[32,32,256]{2,1,0:T(8,128)}, f32[32,32,256]{2,1,0:T(8,128)}, f32[32,32,256]{2,1,0:T(8,128)}) custom-call(f32[40,2,48,128]{3,2,1,0:T(8,128)S(1)} %get-tuple-element.29.now, f32[40,2,48,128]{3,2,1,0:T(8,128)S(1)} %get-tuple-element.30.before, f32[32,2,32,128]{3,2,1,0:T(8,128)S(1)} %get-tuple-element.31.first, ...), custom_call_target="tpu_custom_call" | custom-call | tf_op jit(solution)/shard_map/last/pallas_call | solution.py:635
Async XLA Ops:
  0.6 1.0 %copy-start.1 = (f32[1,128,4,128]{3,2,1,0:T(4,128)S(1)}, f32[1,128,4,128]{3,2,1,0:T(4,128)}, u32[]{:S(2)}) copy-start(f32[1,128,4,128]{3,2,1,0:T(4,128)} %param.11) | copy-start | bytes 786436
  1.6 0.8 %copy-start.2 = (s32[1,128,128]{2,1,0:T(8,128)S(1)}, s32[1,128,128]{2,1,0:T(8,128)}, u32[]{:S(2)}) copy-start(s32[1,128,128]{2,1,0:T(8,128)} %param.12) | copy-start | bytes 196612
  2.4 0.7 copy-start.3
  45.6 21.8 %copy-start = (f32[4,32,32,256]{3,2,1,0:T(8,128)S(1)}, f32[4,32,32,256]{3,2,1,0:T(8,128)}, u32[]{:S(2)}) copy-start(f32[4,32,32,256]{3,2,1,0:T(8,128)} %snapshots.1) | copy-start | bytes 12582916

commit v6 on v5

--- a/solution.py
+++ b/solution.py
@@ -91,29 +91,8 @@
             pl.when(self.there[d])(lambda: self.copies[d].wait_send())
 
 
-def field_landings(field):
-    xs, ys = pl.ds(4, 32), pl.ds(8, 32)
-    return (
-        field.at[xs, :, pl.ds(40, 4), :], field.at[xs, :, pl.ds(4, 4), :],
-        field.at[pl.ds(36, 4), :, ys, :], field.at[pl.ds(0, 4), :, ys, :],
-    )
-
-
 def side_landings(xside, yside):
     return yside.at[1, :, :, pl.ds(8, 4), :], yside.at[0, :, :, pl.ds(4, 4), :], xside.at[1], xside.at[0]
-
-
-def clear_field_edges(field):
-    a, b = lax.axis_index("gx"), lax.axis_index("gy")
-    for edge, low in ((a == 0, 0), (a == NX - 1, 36)):
-        @pl.when(edge)
-        def _():
-            field[pl.ds(low, 4)] = jnp.zeros((4,) + FIELD[1:], jnp.float32)
-
-    for edge, low in ((b == 0, 0), (b == NY - 1, 40)):
-        @pl.when(edge)
-        def _():
-            field[:, :, pl.ds(low, 8), :] = jnp.zeros((40, 2, 8, 128), jnp.float32)
 
 
 def clear_halo(field):
@@ -160,7 +139,7 @@
 def deliver_kernel(
     traces, offsets_hbm, live_hbm, pressure_hbm, previous_hbm, courant_hbm,
     values_out, hom, pressure, courant,
-    offsets, live, slots, previous, mid_values0, mid_values1, field, zterm, dz,
+    offsets, live, slots, previous, mid_values0, mid_values1, field, zterm, dz, xside, yside,
     load_sem, local_sem, send1, recv1, send2, recv2, send3, recv3, send4, recv4, hsend, hrecv,
 ):
     a, b = lax.axis_index("gx"), lax.axis_index("gy")
@@ -188,7 +167,8 @@
     code = (((cells >> 7) * 4 + margin) << 8) | jnp.where(lane < counts, cells & 127, 255)
     slots[:, :, :, 4] = code.astype(jnp.float32).reshape(8, 2, NY, 1, 128)
     loads[5].wait()
-    clear_field_edges(field)
+    clear_halo(field)
+    clear_sides(xside, yside)
     pl.semaphore_wait(sem, len(peers))
 
     core, pair = lax.rem(a, 2), a // 2
@@ -260,7 +240,7 @@
         return 0
 
     lax.fori_loop(0, 32, load, 0)
-    halo = Halo(field, field_landings(field), (hsend, hrecv), 0)
+    halo = Halo(field, side_landings(xside, yside), (hsend, hrecv), 0)
     halo.start()
 
     dz[...] = z_matrix()
@@ -287,7 +267,6 @@
         for copy in own_second:
             copy.start()
 
-    halo.wait()
     loads[3].wait()
     loads[4].wait()
 
@@ -302,6 +281,29 @@
         return 0
 
     lax.fori_loop(0, 32, step, 0)
+    halo.wait()
+
+    def add(x, half, tile, terms):
+        rows = pl.ds(tile * 8, 8)
+        more = courant[x, rows, pl.ds(half * 128, 128)] * terms
+        hom[x, half, rows, :] = hom[x, half, rows, :] + more
+
+    def y_faces(x, _):
+        for half in range(2):
+            for tile in (0, 3):
+                add(x, half, tile, y_face_terms(yside, x, half, tile))
+        return 0
+
+    def x_faces(tile, _):
+        for half in range(2):
+            for side in range(2):
+                for layer in range(4):
+                    x = layer if side == 0 else 31 - layer
+                    add(x, half, tile, x_face_terms(xside, side, layer, half, tile))
+        return 0
+
+    lax.fori_loop(0, 32, y_faces, 0)
+    lax.fori_loop(0, 4, x_faces, 0)
 
     for copy in gy_first:
         copy.wait_send()
@@ -568,6 +570,8 @@
             pltpu.VMEM(FIELD, f32),
             pltpu.VMEM(BLOCK, f32),
             pltpu.VMEM((256, 256), f32),
+            pltpu.VMEM(xside, f32),
+            pltpu.VMEM(yside, f32),
             dma((6,)),
             dma((4, 1)),
             dma((NY - 1, 1)),

time: 69.8 us -> 69.7 us (level)
  no operation moved by 1% of the time
where the time goes in v6:
time: 69.7 us; the launch traced here: 69.1 us
  Pallas kernels  65.9 us (95%)
  local copies, waits for them, and re-layouts  2.44 us (4%)
    pallas_call x1, Pallas kernels, local(): pl.pallas_call(deliver_kernel, out_shape=(jax.ShapeDtypeStruct((NX, NY, 5...  21.8 us
    pallas_call x1, Pallas kernels, local(): pl.pallas_call(steps_kernel, out_shape=(wide, wide, jax.ShapeDtypeStruct(...  21.8 us
    pallas_call x1, Pallas kernels, local(): pl.pallas_call(scatter_kernel, out_shape=(jax.ShapeDtypeStruct((ROWS, 128...  20.6 us
    unnamed x8, local copies, waits for them, and re-layouts  2.44 us
    pallas_call x1, Pallas kernels, local(): pl.pallas_call(last_kernel, out_shape=(block, block, block), in_specs=[vm...  1.74 us

profile of v6, /device:TPU:6, one launch (start us, length us, event | category | flops | bytes accessed | tf_op | source)
XLA Modules:
  0.0 69.1 jit_solution(4710700438295756848)
XLA Ops:
  0.6 0.0 copy-start.1
  0.6 0.9 %copy-done.1 = f32[1,128,4,128]{3,2,1,0:T(4,128)S(1)} copy-done((f32[1,128,4,128]{3,2,1,0:T(4,128)S(1)}, f32[1,128,4,128]{3,2,1,0:T(4,128)}, u32[]{:S(2)}) %copy-start.1) | copy-done | bytes 262168
  1.6 0.0 copy-start.2
  1.6 0.8 %copy-done.2 = s32[1,128,128]{2,1,0:T(8,128)S(1)} copy-done((s32[1,128,128]{2,1,0:T(8,128)S(1)}, s32[1,128,128]{2,1,0:T(8,128)}, u32[]{:S(2)}) %copy-start.2) | copy-done | bytes 65560
  2.4 0.0 copy-start.3
  2.4 0.7 copy-done.3
  3.1 21.8 %deliver.1 = (f32[16,8,5,1,128]{4,3,2,1,0:T(1,128)S(1)}, f32[32,2,32,128]{3,2,1,0:T(8,128)S(1)}, f32[32,32,256]{2,1,0:T(8,128)S(1)}, f32[32,32,256]{2,1,0:T(8,128)S(1)}) custom-call(f32[8,2,8,4,1,128]{5,4,3,2,1,0:T(1,128)S(1)} %bitcast.4, s32[128,128]{1,0:T(8,128)S(1)} %bitcast.5, s32[1,128]{1,0:T(1,128)S(1)} %copy-done.3, f32[32,32,256]{2,1,0:T(8,128)} %pressure_hbm.1, ...), custom_call_target="tpu_custom_call" | custom-call | tf_op jit(solution)/shard_map/deliver/pallas_call | solution.py:553
  24.9 20.6 %scatter.1 = (f32[8208,128]{1,0:T(8,128)S(1)}, f32[8208,128]{1,0:T(8,128)S(1)}, f32[8208,128]{1,0:T(8,128)S(1)}, f32[8208,128]{1,0:T(8,128)S(1)}, f32[8208,128]{1,0:T(8,128)S(1)}, /*index=5*/f32[8208,128]{1,0:T(8,128)S(1)}) custom-call(f32[640,128]{1,0:T(8,128)S(1)} %bitcast.3), custom_call_target="tpu_custom_call" | custom-call | tf_op jit(solution)/shard_map/scatter/pallas_call | solution.py:596
  45.5 0.0 copy-start
  45.6 21.8 %steps.1 = (f32[40,2,48,128]{3,2,1,0:T(8,128)S(1)}, f32[40,2,48,128]{3,2,1,0:T(8,128)S(1)}, f32[32,2,32,128]{3,2,1,0:T(8,128)S(1)}, f32[32,32,256]{2,1,0:T(8,128...) custom-call(f32[8208,128]{1,0:T(8,128)S(1)} %get-tuple-element.20.refs_0_, ...), custom_call_target="tpu_custom_call" | custom-call | tf_op jit(solution)/shard_map/steps/pallas_call | solution.py:613
  67.3 0.0 copy-done
  67.3 1.7 %last.1 = (f32[32,32,256]{2,1,0:T(8,128)}, f32[32,32,256]{2,1,0:T(8,128)}, f32[32,32,256]{2,1,0:T(8,128)}) custom-call(f32[40,2,48,128]{3,2,1,0:T(8,128)S(1)} %get-tuple-element.29.now, f32[40,2,48,128]{3,2,1,0:T(8,128)S(1)} %get-tuple-element.30.before, f32[32,2,32,128]{3,2,1,0:T(8,128)S(1)} %get-tuple-element.31.first, ...), custom_call_target="tpu_custom_call" | custom-call | tf_op jit(solution)/shard_map/last/pallas_call | solution.py:639
Async XLA Ops:
  0.6 1.0 %copy-start.1 = (f32[1,128,4,128]{3,2,1,0:T(4,128)S(1)}, f32[1,128,4,128]{3,2,1,0:T(4,128)}, u32[]{:S(2)}) copy-start(f32[1,128,4,128]{3,2,1,0:T(4,128)} %param.11) | copy-start | bytes 786436
  1.6 0.8 %copy-start.2 = (s32[1,128,128]{2,1,0:T(8,128)S(1)}, s32[1,128,128]{2,1,0:T(8,128)}, u32[]{:S(2)}) copy-start(s32[1,128,128]{2,1,0:T(8,128)} %param.12) | copy-start | bytes 196612
  2.4 0.7 copy-start.3
  45.5 21.8 %copy-start = (f32[4,32,32,256]{3,2,1,0:T(8,128)S(1)}, f32[4,32,32,256]{3,2,1,0:T(8,128)}, u32[]{:S(2)}) copy-start(f32[4,32,32,256]{3,2,1,0:T(8,128)} %snapshots.1) | copy-start | bytes 12582916
